TPU v7x, 128 devices: a whole 4x4x4 slice. The times are simulated.
128 devices in a mesh: span: 4 (over y_lo, core), tm: 32 (over z, y_hi, x).
Axes of the slice: x: 4, y: 4 (y_hi: 2, y_lo: 2; y = y_hi * 2 + y_lo), z: 4, core: 2. Of those that a mesh axis runs over, the one named last changes fastest.
Arguments:
- window_start: int32 [1], replicated, may hold values from 0 to 3968
- owner_map: int32 [32], replicated, may hold values from 0 to 31, each once
- core: bfloat16 [3, 512, 384, 192], P(None, 'tm', 'span'), may hold values from -6 to 6
- span_factor: bfloat16 [1024, 384], P('span'), may hold values from -0.3125 to 0.3125
- height_factor: bfloat16 [512, 192], replicated, may hold values from -0.4375 to 0.4375
- time_factor: bfloat16 [4096, 512], P(None, 'tm'), may hold values from -0.25 to 0.25
Outputs:
- inlet: bfloat16 [128, 3, 1024, 512], P(None, None, ('span', 'tm'))
Inputs may be any that keep to these rules, and one draw needn't show every extreme that they name: owner_map holds each of 0 to 31 once.
All inputs are finite; a program needn't handle non-finite values.
Results may differ from a plain program's by a relative error of at most 0.0058.
Values may be sent and summed in bfloat16 or wider, within the bound.
No kernel may reach another device: no remote copies, remote signals or barrier semaphores. Data moves between devices by JAX's collectives and lax.ppermute only.
A program may use at most 192 MiB of HBM per device.

v0:
```python
import jax
import jax.numpy as jnp
from jax import lax
from jax.sharding import PartitionSpec as P

PL_DEV = 4


def body(window_start, owner_map, core, span_factor, height_factor, time_factor):
    groups = lax.axis_size("tm")
    count = PL_DEV * groups
    rows = lax.dynamic_slice_in_dim(time_factor, window_start[0], count, 0)
    first = lax.psum_scatter(
        jnp.einsum("tr,crab->tcab", rows, core, preferred_element_type=jnp.float32),
        "tm",
        scatter_dimension=0,
        tiled=True,
    ).astype(jnp.bfloat16)
    second = jnp.einsum(
        "tcab,hb->tcah", first, height_factor, preferred_element_type=jnp.float32
    ).astype(jnp.bfloat16)
    local_span = span_factor.shape[0]
    planes = jnp.einsum(
        "sa,tcah->tcsh",
        span_factor,
        lax.all_gather(second, "span", axis=2, tiled=True),
        preferred_element_type=jnp.float32,
    ).astype(jnp.bfloat16)
    tiles = jnp.arange(groups, dtype=jnp.int32)
    owned = jnp.sum(jnp.where(owner_map[:, None] == tiles[None, :], tiles[:, None], 0), axis=0)
    tile_rows = local_span // groups
    blocks = planes.reshape(planes.shape[0], planes.shape[1], groups, tile_rows, planes.shape[3])
    blocks = jnp.take(blocks, owned, axis=2)
    moved = lax.all_to_all(blocks, "tm", split_axis=2, concat_axis=0, tiled=True)
    return moved.reshape(moved.shape[0], moved.shape[1], tile_rows, moved.shape[4])


def solution(mesh):
    in_specs = (P(), P(), P(None, "tm", "span", None), P("span", None), P(), P(None, "tm"))
    out_specs = P(None, None, ("span", "tm"), None)
    return jax.shard_map(body, mesh=mesh, in_specs=in_specs, out_specs=out_specs, check_vma=False)
```

profile of v0, /device:TPU:1, one launch (start us, length us, event | category | flops | bytes accessed | tf_op | source)
XLA Modules:
  0.0 551.2 jit_solution(765617544401939458)
XLA Ops:
  6.5 0.0 copy-start
  6.5 0.0 reduce-scatter.2.cloned.1.call-start
  7.3 0.9 copy-done
  8.2 15.5 %fusion = f32[128,3,96,192]{3,0,2,1:T(8,128)} fusion(bf16[3,16,96,192]{3,2,1,0:T(8,128)(2,1)S(1)} %copy-done, bf16[4096,16]{0,1:T(8,128)(2,1)} %param.11, s32[]{:T(128)S(6)} %select_n.29), kind=kOutput, calls=%fused_computation.3 | convolution fusion | flops 226492416 | bytes 30085124 | tf_op jit(solution)/shard_map/tr,crab->tcab/dot_general | solution.py:14
  23.7 35.3 %copy.10 = f32[128,3,96,192]{3,2,1,0:T(8,128)} copy(f32[128,3,96,192]{3,0,2,1:T(8,128)} %fusion) | data formatting | bytes 56623104 | tf_op jit(solution)/shard_map/tr,crab->tcab/dot_general | solution.py:14
  59.0 0.0 copy-start.2
  59.0 0.0 reduce-scatter.2.cloned.1.call-update
  59.0 0.0 copy-start.4
  59.0 0.0 copy-start.3
  59.1 0.0 all-gather.2.cloned.1.call-start
  59.1 367.8 %reduce-scatter.2.cloned.1.call-done = f32[4,3,96,192]{3,2,1,0:T(8,128)} async-done(((f32[128,3,96,192]{3,2,1,0:T(8,128)}), f32[4,3,96,192]{3,2,1,0:T(8,128)}) %reduce-scatter.2.cloned.1.call-update) | async-done | bytes 884752 | tf_op jit(solution)/shard_map/reduce_scatter | solution.py:13
  427.0 0.0 copy-done.2
  427.0 2.7 convolution_convert_fusion
  429.7 0.0 all-gather.2.cloned.1.call-update
  429.7 0.0 copy-done.4
  429.7 0.1 select_reduce_fusion
  429.9 49.9 %all-gather.2.cloned.1.call-done = bf16[4,3,384,512]{3,2,1,0:T(8,128)(2,1)} async-done(((bf16[4,3,96,512]{3,2,1,0:T(8,128)(2,1)}), bf16[4,3,384,512]{3,2,1,0:T(8,128)(2,1)}) %all-gather.2.cloned.1.call-update) | async-done | bytes 4718608 | tf_op jit(solution)/shard_map/all_gather | solution.py:26
  479.7 0.0 copy-done.3
  479.7 5.8 %convert_bitcast_fusion = bf16[4,3,32,8,512]{4,3,2,1,0:T(8,128)(2,1)} fusion(bf16[4,3,384,512]{3,2,1,0:T(8,128)(2,1)} %all-gather.2.cloned.1.call-done, bf16[256,384]{1,0:T(8,128)(2,1)S(1)} %copy-done.3), kind=kOutput, calls=%fused_computation.2 | convolution fusion | flops 1209532416 | bytes 8060928 | tf_op jit(solution)/shard_map/sa,tcah->tcsh/dot_general | solution.py:23
  485.5 4.3 gather_fusion
  489.8 2.3 select_bitcast_fusion
  492.1 49.5 %all_to_all.15 = bf16[4,3,32,8,512]{4,3,1,0,2:T(8,128)(2,1)S(1)} all-to-all(bf16[4,3,32,8,512]{4,3,1,0,2:T(8,128)(2,1)S(1)} %select_bitcast_fusion), channel_id=1, replica_groups=mesh['span'=4,'tm'=32] {'tm'}, dimensions={2} | all-to-all | bytes 6291456 | tf_op jit(solution)/shard_map/all_to_all | solution.py:34
  541.6 0.0 copy-start.1
  541.6 1.7 copy.18
  543.2 1.1 copy-done.1
  (3 shorter events, 0.0 us)
Async XLA Ops:
  6.5 1.7 copy-start
  6.5 420.4 %reduce-scatter.2.cloned.1.call-start = ((), (), s32[]{:S(2)}) async-start(), calls=%async_computation.2 | async-start | bytes 38928384 | tf_op jit(solution)/shard_map/reduce_scatter | solution.py:13
  59.0 367.9 %copy-start.2 = (bf16[512,192]{0,1:T(8,128)(2,1)S(1)}, bf16[512,192]{0,1:T(8,128)(2,1)}, u32[]{:S(2)}) copy-start(bf16[512,192]{0,1:T(8,128)(2,1)} %param.10) | copy-start | bytes 589828
  59.0 370.7 %copy-start.4 = (s32[32]{0:T(128)S(1)}, s32[32]{0:T(128)}, u32[]{:S(2)}) copy-start(s32[32]{0:T(128)} %param.7) | copy-start | bytes 388
  59.0 420.7 %copy-start.3 = (bf16[256,384]{1,0:T(8,128)(2,1)S(1)}, bf16[256,384]{1,0:T(8,128)(2,1)}, u32[]{:S(2)}) copy-start(bf16[256,384]{1,0:T(8,128)(2,1)} %param.9) | copy-start | bytes 589828
  59.1 420.7 %all-gather.2.cloned.1.call-start = ((), (), s32[]{:S(2)}) async-start(), calls=%async_computation.3 | async-start | bytes 5898240 | tf_op jit(solution)/shard_map/all_gather | solution.py:26
  541.6 2.8 copy-start.1
Sparse Core Ops, SparseCore 0:
  59.2 367.7 reduce-scatter.1
  429.8 49.8 all-gather.1
where the time goes:
time: 552 us; the launch traced here: 551 us
  waiting for transfers between devices  418 us (76%)
  blocking collectives  49.5 us (9%)
  local copies, waits for them, and re-layouts  43.3 us (8%)
  matrix products  24 us (4%)
  between operations  14.3 us (3%)
    reduce_scatter x1, waiting for transfers between devices, body(): lax.psum_scatter(jnp.einsum('tr,crab->tcab', rows, core, preferred_elemen...  368 us
    all_gather x1, waiting for transfers between devices, body(): lax.all_gather(second, 'span', axis=2, tiled=True)  49.9 us
    all_to_all x1, blocking collectives, body(): lax.all_to_all(blocks, 'tm', split_axis=2, concat_axis=0, tiled=True)  49.5 us
    dot_general x1, local copies, waits for them, and re-layouts, body(): jnp.einsum('tr,crab->tcab', rows, core, preferred_element_type=jnp.float32)  35.3 us
    dot_general x1, matrix products, body(): jnp.einsum('tr,crab->tcab', rows, core, preferred_element_type=jnp.float32)  15.5 us
  transfers between devices with their start and end apart: 2, of which 2 were waited for; matrix products, arithmetic and copies ran while one was open for 0% of the time, Pallas kernels for 0%

commit v1 on v0

v1 whole, which is shorter than its diff:
```python
import jax
import jax.numpy as jnp
from jax import lax
from jax.experimental import pallas as pl
from jax.experimental.pallas import tpu as pltpu
from jax.sharding import PartitionSpec as P

AXES = ("span", "tm")
PLANES = 128
DEV = 128
TM = 32
SPAN_DEV = 4
R_LOC = 16
A_LOC = 96
HALF = A_LOC // 2
B = 192
SEND1 = 72
SEND2 = 40
F32 = jnp.float32
BF16 = jnp.bfloat16
LIMIT = pltpu.CompilerParams(vmem_limit_bytes=48 * 1024 * 1024)
VMEM = pl.BlockSpec(memory_space=pltpu.VMEM)


def deal_kernel(core_ref, rows_ref, out_ref, turned):
    eye = (
        lax.broadcasted_iota(jnp.int32, (B, B), 0) == lax.broadcasted_iota(jnp.int32, (B, B), 1)
    ).astype(BF16)
    lane = lax.broadcasted_iota(jnp.int32, (1, 1, 128), 2)
    rows = rows_ref[...].astype(F32)
    turned[...] = jnp.zeros_like(turned)
    for c in range(3):
        for r in range(R_LOC):
            turned[:, r, :A_LOC] = lax.dot_general(
                eye, core_ref[c, r], (((1,), (1,)), ((), ())), preferred_element_type=F32
            )
        full = B if c < 2 else B - 64
        blocks = full // 4
        first = c * (B // 4)

        def put(i, carry, first=first):
            for q in range(4):
                block = jnp.where(lane[0] < A_LOC, turned[4 * i + q], rows[q])
                out_ref[first + i, R_LOC * q : R_LOC * (q + 1), :] = block.astype(BF16)
            return carry

        lax.fori_loop(0, blocks, put, 0, unroll=4)
    low = turned[128:, :8, :]
    high = turned[128:, 8:, :]
    at_0 = jnp.where(lane < HALF, low, pltpu.roll(high, HALF, 2))
    at_1 = jnp.where(lane < HALF, pltpu.roll(low, 128 - HALF, 2), high)

    both = jnp.concatenate([at_0[:, None], at_1[:, None]], axis=1).reshape(DEV, 8, 128)
    out_ref[:, 64:, :] = both.astype(BF16)


def middle_kernel(got_ref, span_ref, out_ref, firsts):
    lane = lax.broadcasted_iota(jnp.int32, (1, 1, 128), 2)
    lane2 = lane[0]
    w = jnp.zeros((TM, R_LOC, 128), F32)
    for q in range(4):
        piece = got_ref[:TM, R_LOC * q : R_LOC * (q + 1), :].astype(F32)
        piece = pltpu.roll(piece, (32 * q - 96) % 128, 2)
        w = jnp.where((lane >= 32 * q) & (lane < 32 * q + 32), piece, w)
    whole = w.reshape(TM * R_LOC, 128).T.astype(BF16)
    low = w[:, :8].reshape(TM * 8, 128).T.astype(BF16)
    high = w[:, 8:].reshape(TM * 8, 128).T.astype(BF16)
    odd = lax.rem(lax.axis_index("tm"), 2) == 1
    for g in range(SPAN_DEV):
        at = slice(g * 128, (g + 1) * 128)
        for q in range(4):
            x = got_ref[TM * g : TM * (g + 1), R_LOC * q : R_LOC * (q + 1), :].reshape(TM * R_LOC, 128)
            firsts[q, :, at] = jnp.dot(whole, x, preferred_element_type=F32).astype(BF16)
        x = got_ref[TM * g : TM * (g + 1), 64:, :].astype(F32).reshape(TM * 8, 128).astype(BF16)
        fa = jnp.dot(low, x, preferred_element_type=F32)
        fb = jnp.dot(high, x, preferred_element_type=F32)
        even_sum = jnp.where(lane2 < HALF, fa + pltpu.roll(fb, 128 - HALF, 1), 0.0)
        odd_sum = jnp.where((lane2 >= HALF) & (lane2 < A_LOC), pltpu.roll(fa, HALF, 1) + fb, 0.0)
        firsts[4, :, at] = jnp.where(odd, odd_sum, even_sum).astype(BF16)
    for q in range(5):
        z = lax.dot_general(
            span_ref[...], firsts[q], (((1,), (1,)), ((), ())), preferred_element_type=F32
        )
        out_ref[:, 8 * q : 8 * (q + 1), :] = z.reshape(DEV, 8, 128).astype(BF16)


def height_kernel(got_ref, height_ref, tail_ref, out_ref, wide, rows):
    for c in range(3):
        if c < 2:
            x = got_ref[48 * c : 48 * (c + 1), :32, :].astype(F32)
            wide[:B] = x.reshape(B, 8, 128)
            depth = B
            factor = height_ref[...]
        else:
            wide[:128] = got_ref[96:, :32, :].astype(F32).reshape(128, 8, 128)
            wide[128:] = got_ref[:, 32:, :].astype(F32)
            depth = 256
            factor = tail_ref[...]
        for s in range(8):
            rows[:, s, :depth] = wide[:depth, s, :].T
        x = rows[:, :, :depth].reshape(PLANES * 8, depth).astype(BF16)
        y = jnp.dot(x, factor, preferred_element_type=F32)
        out_ref[:, c] = y.reshape(PLANES, 8, 512).astype(BF16)


def body(window_start, owner_map, core, span_factor, height_factor, time_factor):
    rows = lax.dynamic_slice_in_dim(time_factor, window_start[0], PLANES, 0)
    quarters = jnp.pad(rows.T.reshape(R_LOC, 4, 32).transpose(1, 0, 2), ((0, 0), (0, 0), (A_LOC, 0)))
    sent = pl.pallas_call(
        deal_kernel,
        out_shape=jax.ShapeDtypeStruct((DEV, SEND1, 128), BF16),
        in_specs=[VMEM, VMEM],
        out_specs=VMEM,
        scratch_shapes=[pltpu.VMEM((B, R_LOC, 128), F32)],
        compiler_params=LIMIT,
        name="deal",
    )(core, quarters)
    got = lax.all_to_all(sent, AXES, 0, 0, tiled=True)

    tiles = jnp.arange(TM, dtype=jnp.int32)
    owned = jnp.sum(jnp.where(owner_map[:, None] == tiles[None, :], tiles[:, None], 0), axis=0)
    span = jnp.take(span_factor.reshape(TM, 8, SPAN_DEV * A_LOC), owned, axis=0)
    span = lax.all_gather(span.reshape(TM * 8, SPAN_DEV * A_LOC), "span", axis=0, tiled=True)
    span = jnp.pad(span.reshape(8 * DEV, SPAN_DEV, A_LOC), ((0, 0), (0, 0), (0, 128 - A_LOC)))
    span = span.reshape(8 * DEV, SPAN_DEV * 128)

    sent = pl.pallas_call(
        middle_kernel,
        out_shape=jax.ShapeDtypeStruct((DEV, SEND2, 128), BF16),
        in_specs=[VMEM, VMEM],
        out_specs=VMEM,
        scratch_shapes=[pltpu.VMEM((5, PLANES, SPAN_DEV * 128), BF16)],
        compiler_params=LIMIT,
        name="middle",
    )(got, span)
    got = lax.all_to_all(sent, AXES, 0, 0, tiled=True)

    height = height_factor.T
    tail = jnp.concatenate([height[:128], jnp.repeat(height[128:], 2, axis=0)], axis=0)
    return pl.pallas_call(
        height_kernel,
        out_shape=jax.ShapeDtypeStruct((PLANES, 3, 8, 512), BF16),
        in_specs=[VMEM, VMEM, VMEM],
        out_specs=VMEM,
        scratch_shapes=[pltpu.VMEM((256, 8, 128), F32), pltpu.VMEM((PLANES, 8, 256), F32)],
        compiler_params=LIMIT,
        name="height",
    )(got, height, tail)


def solution(mesh):
    in_specs = (P(), P(), P(None, "tm", "span", None), P("span", None), P(), P(None, "tm"))
    out_specs = P(None, None, ("span", "tm"), None)
    return jax.shard_map(body, mesh=mesh, in_specs=in_specs, out_specs=out_specs, check_vma=False)
```

time: 552 us -> 99.1 us (0.18)
  waiting for transfers between devices: 418 us -> 21.7 us
  local copies, waits for them, and re-layouts: 43.3 us -> 12 us
  matrix products: 24 us -> 0 us
  starting transfers between devices: 0.04 us -> 20.6 us
  blocking collectives: 49.5 us -> 32 us
  between operations: 14.3 us -> 0.84 us
  Pallas kernels: 0 us -> 11.2 us
    reduce_scatter x1 -> x0, waiting for transfers between devices: 368 us -> none  [body(): lax.psum_scatter(jnp.einsum('tr,crab->tcab', rows, core, preferred_elemen...]
    all_gather x1 -> x0, waiting for transfers between devices: 49.9 us -> none  [body(): lax.all_gather(second, 'span', axis=2, tiled=True)]
    all_to_all x1 -> x0, blocking collectives: 49.5 us -> none  [body(): lax.all_to_all(blocks, 'tm', split_axis=2, concat_axis=0, tiled=True)]
    dot_general x1 -> x0, local copies, waits for them, and re-layouts: 35.3 us -> none  [body(): jnp.einsum('tr,crab->tcab', rows, core, preferred_element_type=jnp.float32)]
    all_gather x0 -> x1, blocking collectives: none -> 32 us  [body(): lax.all_gather(span.reshape(TM * 8, SPAN_DEV * A_LOC), 'span', axis=0, ti...]
    dot_general x3 -> x0, matrix products: 24 us -> none  [the longest x1 15.5 us: body(): jnp.einsum('tr,crab->tcab', rows, core, preferred_element_type=jnp.float32)]
    all_to_all x0 -> x2, waiting for transfers between devices: none -> 21.7 us  [body(): got = lax.all_to_all(sent, AXES, 0, 0, tiled=True)]
    all_to_all x0 -> x2, starting transfers between devices: none -> 20.6 us  [body(): got = lax.all_to_all(sent, AXES, 0, 0, tiled=True)]
  transfers between devices with their start and end apart: 2 -> 2, of which waited for: 2 -> 1; matrix products, arithmetic and copies ran while one was open for 0% -> 6% of each run, Pallas kernels for 0% -> 0%
where the time goes in v1:
time: 99.1 us; the launch traced here: 98.6 us
  blocking collectives  32 us (32%)
  waiting for transfers between devices  21.7 us (22%)
  starting transfers between devices  20.6 us (21%)
  local copies, waits for them, and re-layouts  12 us (12%)
  Pallas kernels  11.2 us (11%)
    all_gather x1, blocking collectives, body(): lax.all_gather(span.reshape(TM * 8, SPAN_DEV * A_LOC), 'span', axis=0, ti...  32 us
    all_to_all x2, waiting for transfers between devices, body(): got = lax.all_to_all(sent, AXES, 0, 0, tiled=True)  21.7 us
    all_to_all x2, starting transfers between devices, body(): got = lax.all_to_all(sent, AXES, 0, 0, tiled=True)  20.6 us
    unnamed x14, local copies, waits for them, and re-layouts  5.36 us
    pallas_call x1, Pallas kernels, body(): pl.pallas_call(height_kernel, out_shape=jax.ShapeDtypeStruct((PLANES, 3,...  4.9 us
    pallas_call x1, Pallas kernels, body(): pl.pallas_call(deal_kernel, out_shape=jax.ShapeDtypeStruct((DEV, SEND1, 1...  3.91 us
    pallas_call x1, Pallas kernels, body(): pl.pallas_call(middle_kernel, out_shape=jax.ShapeDtypeStruct((DEV, SEND2,...  2.4 us
    reshape x1, local copies, waits for them, and re-layouts, body(): span = span.reshape(8 * DEV, SPAN_DEV * 128)  2.28 us
  transfers between devices with their start and end apart: 2, of which 1 were waited for; matrix products, arithmetic and copies ran while one was open for 6% of the time, Pallas kernels for 0%

profile of v1, /device:TPU:1, one launch (start us, length us, event | category | flops | bytes accessed | tf_op | source)
XLA Modules:
  0.0 98.6 jit_solution(18353878151645948462)
XLA Ops:
  0.0 0.0 copy-start
  0.7 0.8 dynamic-slice_bitcast_fusion
  1.5 0.1 reshape.37
  1.6 0.1 pad.8.rows_ref
  1.7 0.0 copy-start.4
  1.7 1.7 %copy-done.4 = bf16[3,16,96,192]{3,2,1,0:T(8,128)(2,1)S(1)} copy-done((bf16[3,16,96,192]{3,2,1,0:T(8,128)(2,1)S(1)}, bf16[3,16,96,192]{3,2,1,0:T(8,128)(2,1)}, u32[]{:S(2)}) %copy-start.4) | copy-done | bytes 1769496
  3.3 3.9 %deal.1 = bf16[128,72,128]{2,1,0:T(8,128)(2,1)S(1)} custom-call(bf16[3,16,96,192]{3,2,1,0:T(8,128)(2,1)S(1)} %copy-done.4, bf16[4,16,128]{2,1,0:T(8,128)(2,1)S(1)} %pad.8.rows_ref), custom_call_target="tpu_custom_call" | custom-call | tf_op jit(solution)/shard_map/deal/pallas_call | solution.py:109
  7.3 0.0 copy-start.1
  7.3 1.4 %copy-done.1 = bf16[128,72,128]{2,1,0:T(8,128)(2,1)} copy-done((bf16[128,72,128]{2,1,0:T(8,128)(2,1)}, bf16[128,72,128]{2,1,0:T(8,128)(2,1)S(1)}, u32[]{:S(2)}) %copy-start.1) | copy-done | bytes 2359320
  8.7 0.0 copy-start.6
  8.7 11.5 %all-to-all-start = ((bf16[128,72,128]{2,1,0:T(8,128)(2,1)}), bf16[128,72,128]{2,1,0:T(8,128)(2,1)S(1)}, u32[]{:S(2)}, u32[]{:S(2)}) async-start(bf16[128,72,128]{2,1,0:T(8,128)(2,1)} %copy-done.1), calls=%async_computation | async-start | bytes 4718592 | tf_op jit(solution)/shard_map/all_to_all | solution.py:118
  20.2 0.0 copy-done.6
  20.2 0.1 select_reduce_fusion
  20.3 0.1 broadcast_in_dim.34
  20.4 0.1 broadcast_in_dim.35
  20.5 0.0 copy-done
  20.5 0.6 gather_fusion
  21.1 0.1 bitcast_select_fusion
  21.2 32.0 %all_gather.3 = bf16[1024,384]{1,0:T(8,128)(2,1)} all-gather(bf16[256,384]{1,0:T(8,128)(2,1)S(1)} %bitcast_select_fusion), channel_id=1, replica_groups=mesh['span'=4,'tm'=32] {'span'}, dimensions={0}, use_global_device_ids=true | all-gather | bytes 983040 | tf_op jit(solution)/shard_map/all_gather | solution.py:123
  53.2 1.4 %copy.13 = bf16[1024,384]{0,1:T(8,128)(2,1)S(1)} copy(bf16[1024,384]{1,0:T(8,128)(2,1)} %all_gather.3) | data formatting | bytes 1572864 | tf_op jit(solution)/shard_map/all_gather | solution.py:123
  54.6 1.1 %pad.9 = bf16[1024,4,128]{0,2,1:T(8,128)(2,1)} pad(bf16[1024,4,96]{0,2,1:T(8,128)(2,1)S(1)} %bitcast.24, bf16[]{:T(256)} %constant.17.clone.1), padding=0_0x0_0x0_32 | pad | bytes 1835010 | tf_op jit(solution)/shard_map/jit(_pad)/pad | solution.py:124
  55.7 2.3 %copy.15.span_ref = bf16[1024,512]{1,0:T(8,128)(2,1)} copy(bf16[1024,512]{0,1:T(8,128)(2,1)} %bitcast.23) | data formatting | bytes 2097152 | tf_op jit(solution)/shard_map/reshape | solution.py:125
  58.0 0.0 all-to-all-done.got_ref
  58.0 0.0 copy-start.3
  58.0 1.2 %copy-done.3 = bf16[1024,512]{1,0:T(8,128)(2,1)S(1)} copy-done((bf16[1024,512]{1,0:T(8,128)(2,1)S(1)}, bf16[1024,512]{1,0:T(8,128)(2,1)}, u32[]{:S(2)}) %copy-start.3) | copy-done | bytes 1048600
  59.2 2.4 %middle.1 = bf16[128,40,128]{2,1,0:T(8,128)(2,1)S(1)} custom-call(bf16[128,72,128]{2,1,0:T(8,128)(2,1)S(1)} %all-to-all-done.got_ref, bf16[1024,512]{1,0:T(8,128)(2,1)S(1)} %copy-done.3), custom_call_target="tpu_custom_call" | custom-call | tf_op jit(solution)/shard_map/middle/pallas_call | solution.py:127
  61.6 0.0 copy-start.2
  61.6 1.0 %copy-done.2 = bf16[128,40,128]{2,1,0:T(8,128)(2,1)} copy-done((bf16[128,40,128]{2,1,0:T(8,128)(2,1)}, bf16[128,40,128]{2,1,0:T(8,128)(2,1)S(1)}, u32[]{:S(2)}) %copy-start.2) | copy-done | bytes 1310744
  62.7 0.0 copy-start.5
  62.7 9.1 %all-to-all-start.1 = ((bf16[128,40,128]{2,1,0:T(8,128)(2,1)}), bf16[128,40,128]{2,1,0:T(8,128)(2,1)S(1)}, u32[]{:S(2)}, u32[]{:S(2)}) async-start(bf16[128,40,128]{2,1,0:T(8,128)(2,1)} %copy-done.2), calls=%async_computation.1 | async-start | bytes 2621440 | tf_op jit(solution)/shard_map/all_to_all | solution.py:136
  71.8 0.0 copy-done.5
  71.8 0.1 broadcast_in_dim.38
  71.9 0.1 reshape.41
  72.0 21.7 %all-to-all-done.1.got_ref = bf16[128,40,128]{2,1,0:T(8,128)(2,1)S(1)} async-done(((bf16[128,40,128]{2,1,0:T(8,128)(2,1)}), bf16[128,40,128]{2,1,0:T(8,128)(2,1)S(1)}, u32[]{:S(2)}, u32[]{:S(2)}) %all-to-all-start.1) | async-done | bytes 1310752 | tf_op jit(solution)/shard_map/all_to_all | solution.py:136
  93.7 4.9 %height.1 = bf16[128,3,8,512]{3,2,1,0:T(8,128)(2,1)} custom-call(bf16[128,40,128]{2,1,0:T(8,128)(2,1)S(1)} %all-to-all-done.1.got_ref, bf16[192,512]{1,0:T(8,128)(2,1)S(1)} %bitcast.22, bf16[256,512]{1,0:T(8,128)(2,1)S(1)} %pad_maximum_fusion.tail_ref), custom_call_target="tpu_custom_call" | custom-call | tf_op jit(solution)/shard_map/height/pallas_call | solution.py:140
  (7 shorter events, 0.1 us)
Async XLA Ops:
  0.0 20.5 %copy-start = (bf16[256,384]{1,0:T(8,128)(2,1)S(1)}, bf16[256,384]{1,0:T(8,128)(2,1)}, u32[]{:S(2)}) copy-start(bf16[256,384]{1,0:T(8,128)(2,1)} %param.9) | copy-start | bytes 589828
  1.7 1.7 %copy-start.4 = (bf16[3,16,96,192]{3,2,1,0:T(8,128)(2,1)S(1)}, bf16[3,16,96,192]{3,2,1,0:T(8,128)(2,1)}, u32[]{:S(2)}) copy-start(bf16[3,16,96,192]{3,2,1,0:T(8,128)(2,1)} %core_ref.1) | copy-start | bytes 5308420
  7.3 1.4 %copy-start.1 = (bf16[128,72,128]{2,1,0:T(8,128)(2,1)}, bf16[128,72,128]{2,1,0:T(8,128)(2,1)S(1)}, u32[]{:S(2)}) copy-start(bf16[128,72,128]{2,1,0:T(8,128)(2,1)S(1)} %deal.1) | copy-start | bytes 7077892
  8.7 11.5 %copy-start.6 = (s32[32]{0:T(128)S(1)}, s32[32]{0:T(128)}, u32[]{:S(2)}) copy-start(s32[32]{0:T(128)} %param.7) | copy-start | bytes 388
  8.7 49.3 %all-to-all-start = ((bf16[128,72,128]{2,1,0:T(8,128)(2,1)}), bf16[128,72,128]{2,1,0:T(8,128)(2,1)S(1)}, u32[]{:S(2)}, u32[]{:S(2)}) async-start(bf16[128,72,128]{2,1,0:T(8,128)(2,1)} %copy-done.1), calls=%async_computation | async-start | bytes 4718592 | tf_op jit(solution)/shard_map/all_to_all | solution.py:118
  58.0 1.2 %copy-start.3 = (bf16[1024,512]{1,0:T(8,128)(2,1)S(1)}, bf16[1024,512]{1,0:T(8,128)(2,1)}, u32[]{:S(2)}) copy-start(bf16[1024,512]{1,0:T(8,128)(2,1)} %copy.15.span_ref) | copy-start | bytes 3145732
  61.6 1.1 %copy-start.2 = (bf16[128,40,128]{2,1,0:T(8,128)(2,1)}, bf16[128,40,128]{2,1,0:T(8,128)(2,1)S(1)}, u32[]{:S(2)}) copy-start(bf16[128,40,128]{2,1,0:T(8,128)(2,1)S(1)} %middle.1) | copy-start | bytes 3932164
  62.7 9.1 %copy-start.5 = (bf16[512,192]{0,1:T(8,128)(2,1)S(1)}, bf16[512,192]{0,1:T(8,128)(2,1)}, u32[]{:S(2)}) copy-start(bf16[512,192]{0,1:T(8,128)(2,1)} %param.10) | copy-start | bytes 589828
  62.7 31.0 %all-to-all-start.1 = ((bf16[128,40,128]{2,1,0:T(8,128)(2,1)}), bf16[128,40,128]{2,1,0:T(8,128)(2,1)S(1)}, u32[]{:S(2)}, u32[]{:S(2)}) async-start(bf16[128,40,128]{2,1,0:T(8,128)(2,1)} %copy-done.2), calls=%async_computation.1 | async-start | bytes 2621440 | tf_op jit(solution)/shard_map/all_to_all | solution.py:136

commit v2 on v0

v2 whole, which is shorter than its diff:
```python
import jax
import jax.numpy as jnp
from jax import lax
from jax.experimental import pallas as pl
from jax.experimental.pallas import tpu as pltpu
from jax.sharding import PartitionSpec as P

AXES = ("span", "tm")
PLANES = 128
WINDOW = 2 * PLANES
DEV = 128
TM = 32
SPAN_DEV = 4
R_LOC = 16
A_LOC = 96
HALF = A_LOC // 2
A_ALL = SPAN_DEV * A_LOC
B = 192
SEND1 = 72
SEND2 = 40
PITCH = R_LOC + 1
PITCH2 = 8 + 1
PARTS = 4
F32 = jnp.float32
BF16 = jnp.bfloat16
MIB = 1024 * 1024
VMEM = pl.BlockSpec(memory_space=pltpu.VMEM)
SMEM = pl.BlockSpec(memory_space=pltpu.SMEM)
HBM = pl.BlockSpec(memory_space=pltpu.HBM)


def lanes(shape):
    return lax.broadcasted_iota(jnp.int32, shape, len(shape) - 1)


def deal_kernel(
    start_ref, owner_ref, core_ref, time_ref, span_ref, out_ref, tiles_ref, held, window, turned, stage, in_sem, time_sem, out_sem
):
    order = (2, 0, 1)
    ins = {c: pltpu.make_async_copy(core_ref.at[c], held.at[c], in_sem.at[c]) for c in order}
    start = start_ref[0]
    base = jnp.minimum(start // 128, (time_ref.shape[1] - WINDOW) // 128)
    window_in = pltpu.make_async_copy(
        time_ref.at[:, pl.ds(pl.multiple_of(base * 128, 128), WINDOW)], window, time_sem
    )
    window_in.start()
    for c in order:
        ins[c].start()
    eye = (
        lax.broadcasted_iota(jnp.int32, (B, B), 0) == lax.broadcasted_iota(jnp.int32, (B, B), 1)
    ).astype(BF16)
    lane = lanes((1, 128))
    for j in range(TM):
        owner = pl.multiple_of(owner_ref[j] * 8, 8)
        tiles_ref[pl.ds(owner, 8), :] = span_ref[8 * j : 8 * (j + 1), :]
    window_in.wait()
    rows = pltpu.roll(window[...].astype(F32), (WINDOW - (start - base * 128)) % WINDOW, 1)[:, :PLANES]
    rows = [pltpu.roll(rows, (A_LOC - 32 * q) % 128, 1) for q in range(4)]
    gap = jnp.zeros((128 - A_LOC, B), BF16)
    outs = []
    for c in order:
        ins[c].wait()
        for r in range(0, R_LOC, 2):
            x = jnp.concatenate([held[c, r], gap, held[c, r + 1], gap], axis=0)
            y = lax.dot_general(eye, x, (((1,), (1,)), ((), ())), preferred_element_type=F32)
            turned[pl.ds(r, B, PITCH), :] = y[:, :128]
            turned[pl.ds(r + 1, B, PITCH), :] = y[:, 128:]
        first = c * (B // 4)
        blocks = 48 if c < 2 else 32
        for b in range(4 * blocks):
            i, q = b // 4, b % 4
            block = jnp.where(lane < A_LOC, turned[pl.ds(PITCH * b, R_LOC), :], rows[q])
            stage[first + i, R_LOC * q : R_LOC * (q + 1), :] = block.astype(BF16)
        if c == 2:
            for j in range(64):
                low = turned[pl.ds(PITCH * (128 + j), 8), :]
                high = turned[pl.ds(PITCH * (128 + j) + 8, 8), :]
                at_0 = jnp.where(lane < HALF, low, pltpu.roll(high, HALF, 1))
                at_1 = jnp.where(lane < HALF, pltpu.roll(low, 128 - HALF, 1), high)
                stage[2 * j, 64:, :] = at_0.astype(BF16)
                stage[2 * j + 1, 64:, :] = at_1.astype(BF16)
        out = pltpu.make_async_copy(
            stage.at[pl.ds(first, blocks)], out_ref.at[pl.ds(first, blocks)], out_sem.at[c]
        )
        out.start()
        outs.append(out)
    for out in outs:
        out.wait()


def middle_kernel(held, span_ref, out_ref, span, firsts, span_sem):
    span_in = pltpu.make_async_copy(span_ref, span, span_sem)
    span_in.start()
    lane3 = lanes((1, 1, 128))
    lane = lanes((1, 128))
    odd = lax.rem(lax.axis_index("tm"), 2) == 1
    for g in range(SPAN_DEV):
        if g == 0:
            w = jnp.zeros((TM, R_LOC, 128), F32)
            for q in range(4):
                piece = held[:TM, R_LOC * q : R_LOC * (q + 1), :].astype(F32)
                piece = pltpu.roll(piece, (32 * q - A_LOC) % 128, 2)
                w = jnp.where((lane3 >= 32 * q) & (lane3 < 32 * q + 32), piece, w)
            whole = w.reshape(TM * R_LOC, 128).T.astype(BF16)
            low = w[:, :8].reshape(TM * 8, 128).T.astype(BF16)
            high = w[:, 8:].reshape(TM * 8, 128).T.astype(BF16)
        for q in range(4):
            x = held[TM * g : TM * (g + 1), R_LOC * q : R_LOC * (q + 1), :].reshape(TM * R_LOC, 128)
            firsts[q, g] = jnp.dot(whole, x, preferred_element_type=F32)
        x = held[TM * g : TM * (g + 1), 64:, :].astype(F32).reshape(TM * 8, 128).astype(BF16)
        fa = jnp.dot(low, x, preferred_element_type=F32)
        fb = jnp.dot(high, x, preferred_element_type=F32)
        even_sum = jnp.where(lane < HALF, fa + pltpu.roll(fb, 128 - HALF, 1), 0.0)
        odd_sum = jnp.where((lane >= HALF) & (lane < A_LOC), pltpu.roll(fa, HALF, 1) + fb, 0.0)
        firsts[4, g] = jnp.where(odd, odd_sum, even_sum)
    packed = []
    for q in range(5):
        f0, f1, f2, f3 = (firsts[q, g] for g in range(SPAN_DEV))
        tiles = (
            jnp.where(lane < 96, f0, pltpu.roll(f1, 96, 1)),
            jnp.where(lane < 64, pltpu.roll(f1, 96, 1), pltpu.roll(f2, 64, 1)),
            jnp.where(lane < 32, pltpu.roll(f2, 64, 1), pltpu.roll(f3, 32, 1)),
        )
        packed.append(jnp.concatenate(tiles, axis=1).astype(BF16))
    packed = jnp.concatenate(packed, axis=0)
    span_in.wait()
    for g in range(SPAN_DEV):
        z = lax.dot_general(
            span[TM * 8 * g : TM * 8 * (g + 1)],
            packed,
            (((1,), (1,)), ((), ())),
            preferred_element_type=F32,
        )
        for q in range(5):
            tile = z[:, 128 * q : 128 * (q + 1)].reshape(TM, 8, 128)
            out_ref[TM * g : TM * (g + 1), 8 * q : 8 * (q + 1), :] = tile.astype(BF16)


def height_kernel(held, height_ref, out_ref, height, wide, rows, stage, height_sem, out_sem):
    height_in = pltpu.make_async_copy(height_ref, height, height_sem)
    height_in.start()
    begins = (0, 48, 96)
    part = PLANES // PARTS
    outs = []
    for c in range(3):
        whole = B if c < 2 else 128
        for b in range(whole):
            source, q = begins[c] + b // 4, b % 4
            wide[c, pl.ds(PITCH2 * b, 8), :] = held[source, 8 * q : 8 * (q + 1), :].astype(F32)
        for b in range(whole, B):
            source = 2 * (b - 128)
            wide[c, pl.ds(PITCH2 * b, 8), :] = held[source, 32:, :].astype(F32) + held[source + 1, 32:, :].astype(F32)
        for s in range(8):
            x = wide.at[c][pl.ds(s, B, PITCH2), :].T
            rows.at[c, 0][pl.ds(s, PLANES, PITCH2), :] = x[:, :128]
            x = jnp.concatenate([x[:, 128:], jnp.zeros((PLANES, 256 - B), F32)], axis=1)
            rows.at[c, 1][pl.ds(s, PLANES, PITCH2), :] = x
        if c == 0:
            height_in.wait()
        for p in range(PARTS):
            x = [
                jnp.concatenate(
                    [rows[c, e, pl.ds(PITCH2 * t, 8), :] for t in range(part * p, part * (p + 1))], axis=0
                )
                for e in range(2)
            ]
            x = jnp.concatenate(x, axis=1)[:, :B].astype(BF16)
            y = jnp.dot(x, height[...], preferred_element_type=F32)
            at = pl.ds(part * p, part)
            stage[c, at] = y.reshape(part, 8, 512).astype(BF16)
            out = pltpu.make_async_copy(stage.at[c, at], out_ref.at[at, c], out_sem.at[PARTS * c + p])
            out.start()
            outs.append(out)
    for out in outs:
        out.wait()


def body(window_start, owner_map, core, span_factor, height_factor, time_factor):
    sent, tiles = pl.pallas_call(
        deal_kernel,
        out_shape=(
            jax.ShapeDtypeStruct((DEV, SEND1, 128), BF16),
            jax.ShapeDtypeStruct((8 * TM, A_ALL), BF16),
        ),
        in_specs=[SMEM, SMEM, HBM, HBM, VMEM],
        out_specs=(HBM, VMEM),
        scratch_shapes=[
            pltpu.VMEM((3, R_LOC, A_LOC, B), BF16),
            pltpu.VMEM((R_LOC, WINDOW), BF16),
            pltpu.VMEM((PITCH * B, 128), F32),
            pltpu.VMEM((DEV, SEND1, 128), BF16),
            pltpu.SemaphoreType.DMA((3,)),
            pltpu.SemaphoreType.DMA,
            pltpu.SemaphoreType.DMA((3,)),
        ],
        compiler_params=pltpu.CompilerParams(vmem_limit_bytes=60 * MIB),
        name="deal",
    )(window_start, owner_map, core, time_factor.T, span_factor)
    got = lax.all_to_all(sent, AXES, 0, 0, tiled=True)
    span = lax.all_gather(tiles, "span", axis=0, tiled=True)
    sent = pl.pallas_call(
        middle_kernel,
        out_shape=jax.ShapeDtypeStruct((DEV, SEND2, 128), BF16),
        in_specs=[VMEM, HBM],
        out_specs=VMEM,
        scratch_shapes=[
            pltpu.VMEM((8 * DEV, A_ALL), BF16),
            pltpu.VMEM((5, SPAN_DEV, PLANES, 128), F32),
            pltpu.SemaphoreType.DMA,
        ],
        compiler_params=pltpu.CompilerParams(vmem_limit_bytes=40 * MIB),
        name="middle",
    )(got, span)
    got = lax.all_to_all(sent, AXES, 0, 0, tiled=True)
    return pl.pallas_call(
        height_kernel,
        out_shape=jax.ShapeDtypeStruct((PLANES, 3, 8, 512), BF16),
        in_specs=[VMEM, HBM],
        out_specs=HBM,
        scratch_shapes=[
            pltpu.VMEM((B, 512), BF16),
            pltpu.VMEM((3, PITCH2 * B, 128), F32),
            pltpu.VMEM((3, 2, PITCH2 * PLANES, 128), F32),
            pltpu.VMEM((3, PLANES, 8, 512), BF16),
            pltpu.SemaphoreType.DMA,
            pltpu.SemaphoreType.DMA((3 * PARTS,)),
        ],
        compiler_params=pltpu.CompilerParams(vmem_limit_bytes=40 * MIB),
        name="height",
    )(got, height_factor.T)


def solution(mesh):
    in_specs = (P(), P(), P(None, "tm", "span", None), P("span", None), P(), P(None, "tm"))
    out_specs = P(None, None, ("span", "tm"), None)
    return jax.shard_map(body, mesh=mesh, in_specs=in_specs, out_specs=out_specs, check_vma=False)
```

time: 552 us -> 86.5 us (0.16)
  waiting for transfers between devices: 418 us -> 0.53 us
  local copies, waits for them, and re-layouts: 43.3 us -> 0.01 us
  matrix products: 24 us -> 0 us
  between operations: 14.3 us -> 0.7 us
  blocking collectives: 49.5 us -> 62.9 us
  starting transfers between devices: 0.04 us -> 11.5 us
  Pallas kernels: 0 us -> 10.6 us
    reduce_scatter x1 -> x0, waiting for transfers between devices: 368 us -> none  [body(): lax.psum_scatter(jnp.einsum('tr,crab->tcab', rows, core, preferred_elemen...]
    all_gather x1 -> x0, waiting for transfers between devices: 49.9 us -> none  [body(): lax.all_gather(second, 'span', axis=2, tiled=True)]
    dot_general x1 -> x0, local copies, waits for them, and re-layouts: 35.3 us -> none  [body(): jnp.einsum('tr,crab->tcab', rows, core, preferred_element_type=jnp.float32)]
    all_gather x0 -> x1, blocking collectives: none -> 32.6 us  [body(): span = lax.all_gather(tiles, 'span', axis=0, tiled=True)]
    dot_general x3 -> x0, matrix products: 24 us -> none  [the longest x1 15.5 us: body(): jnp.einsum('tr,crab->tcab', rows, core, preferred_element_type=jnp.float32)]
    all_to_all x1, blocking collectives: 49.5 us -> 30.3 us  [body(): got = lax.all_to_all(sent, AXES, 0, 0, tiled=True)]
    all_to_all x0 -> x1, starting transfers between devices: none -> 11.5 us  [body(): got = lax.all_to_all(sent, AXES, 0, 0, tiled=True)]
    pallas_call x0 -> x3, Pallas kernels: none -> 10.6 us  [the longest x1 5.82 us: body(): pl.pallas_call(deal_kernel, out_shape=(jax.ShapeDtypeStruct((DEV, SEND1,...]
  transfers between devices with their start and end apart: 2 -> 1, of which waited for: 2 -> 1; matrix products, arithmetic and copies ran while one was open for 0% -> 0% of each run, Pallas kernels for 0% -> 0%
where the time goes in v2:
time: 86.5 us; the launch traced here: 86.2 us
  blocking collectives  62.9 us (73%)
  starting transfers between devices  11.5 us (13%)
  Pallas kernels  10.6 us (12%)
    all_gather x1, blocking collectives, body(): span = lax.all_gather(tiles, 'span', axis=0, tiled=True)  32.6 us
    all_to_all x1, blocking collectives, body(): got = lax.all_to_all(sent, AXES, 0, 0, tiled=True)  30.3 us
    all_to_all x1, starting transfers between devices, body(): got = lax.all_to_all(sent, AXES, 0, 0, tiled=True)  11.5 us
    pallas_call x1, Pallas kernels, body(): pl.pallas_call(deal_kernel, out_shape=(jax.ShapeDtypeStruct((DEV, SEND1,...  5.82 us
    pallas_call x1, Pallas kernels, body(): pl.pallas_call(height_kernel, out_shape=jax.ShapeDtypeStruct((PLANES, 3,...  2.49 us
    pallas_call x1, Pallas kernels, body(): pl.pallas_call(middle_kernel, out_shape=jax.ShapeDtypeStruct((DEV, SEND2,...  2.27 us
  transfers between devices with their start and end apart: 1, of which 1 were waited for; matrix products, arithmetic and copies ran while one was open for 0% of the time, Pallas kernels for 0%

profile of v2, /device:TPU:1, one launch (start us, length us, event | category | flops | bytes accessed | tf_op | source)
XLA Modules:
  0.0 86.2 jit_solution(8804841873656101010)
XLA Ops:
  0.7 5.8 %deal.1 = (bf16[128,72,128]{2,1,0:T(8,128)(2,1)}, bf16[256,384]{1,0:T(8,128)(2,1)}) custom-call(s32[1]{0:T(128)S(6)} %copy.7.start_ref, s32[32]{0:T(128)} %owner_ref.1, bf16[3,16,96,192]{3,2,1,0:T(8,128)(2,1)} %core_ref.1, bf16[16,4096]{1,0:T(8,128)(2,1)} %bitcast.3, bf16[256,384]{1,0:T(8,128)(2,1)} %span_ref.1), custom_call_target="tpu_custom_call" | custom-call | tf_op jit(solution)/shard_map/deal/pallas_call | solution.py:179
  6.5 0.0 copy-start.1
  6.5 11.5 %all-to-all-start = ((bf16[128,72,128]{2,1,0:T(8,128)(2,1)}), bf16[128,72,128]{2,1,0:T(8,128)(2,1)S(1)}, u32[]{:S(2)}, u32[]{:S(2)}) async-start(bf16[128,72,128]{2,1,0:T(8,128)(2,1)} %get-tuple-element.7), calls=%async_computation | async-start | bytes 4718592 | tf_op jit(solution)/shard_map/all_to_all | solution.py:199
  18.0 0.0 copy-done.1
  18.0 32.6 %all_gather.3.span_ref = bf16[1024,384]{1,0:T(8,128)(2,1)S(1)} all-gather(bf16[256,384]{1,0:T(8,128)(2,1)S(1)} %copy-done.1), channel_id=1, replica_groups=mesh['span'=4,'tm'=32] {'span'}, dimensions={0}, use_global_device_ids=true | all-gather | bytes 983040 | tf_op jit(solution)/shard_map/all_gather | solution.py:200
  50.6 0.5 all-to-all-done.held
  51.1 2.3 %middle.1 = bf16[128,40,128]{2,1,0:T(8,128)(2,1)S(1)} custom-call(bf16[128,72,128]{2,1,0:T(8,128)(2,1)S(1)} %all-to-all-done.held, bf16[1024,384]{1,0:T(8,128)(2,1)S(1)} %all_gather.3.span_ref), custom_call_target="tpu_custom_call" | custom-call | tf_op jit(solution)/shard_map/middle/pallas_call | solution.py:201
  53.4 0.0 copy-start
  53.4 30.3 %all_to_all.10.held = bf16[128,40,128]{2,1,0:T(8,128)(2,1)S(1)} all-to-all(bf16[128,40,128]{2,1,0:T(8,128)(2,1)S(1)} %middle.1), channel_id=1, replica_groups=mesh['span'=4,'tm'=32] {'span','tm'}, dimensions={0} | all-to-all | bytes 2621440 | tf_op jit(solution)/shard_map/all_to_all | solution.py:214
  83.7 0.0 copy-done
  83.7 2.5 %height.1 = bf16[128,3,8,512]{3,2,1,0:T(8,128)(2,1)} custom-call(bf16[128,40,128]{2,1,0:T(8,128)(2,1)S(1)} %all_to_all.10.held, bf16[192,512]{1,0:T(8,128)(2,1)S(1)} %bitcast.2), custom_call_target="tpu_custom_call" | custom-call | tf_op jit(solution)/shard_map/height/pallas_call | solution.py:215
Async XLA Ops:
  6.5 11.5 %copy-start.1 = (bf16[256,384]{1,0:T(8,128)(2,1)S(1)}, bf16[256,384]{1,0:T(8,128)(2,1)}, u32[]{:S(2)}) copy-start(bf16[256,384]{1,0:T(8,128)(2,1)} %get-tuple-element.8) | copy-start | bytes 589828
  6.5 44.6 %all-to-all-start = ((bf16[128,72,128]{2,1,0:T(8,128)(2,1)}), bf16[128,72,128]{2,1,0:T(8,128)(2,1)S(1)}, u32[]{:S(2)}, u32[]{:S(2)}) async-start(bf16[128,72,128]{2,1,0:T(8,128)(2,1)} %get-tuple-element.7), calls=%async_computation | async-start | bytes 4718592 | tf_op jit(solution)/shard_map/all_to_all | solution.py:199
  53.4 30.3 %copy-start = (bf16[512,192]{0,1:T(8,128)(2,1)S(1)}, bf16[512,192]{0,1:T(8,128)(2,1)}, u32[]{:S(2)}) copy-start(bf16[512,192]{0,1:T(8,128)(2,1)} %param.10) | copy-start | bytes 589828

commit v3 on v2

v3 whole, which is shorter than its diff:
```python
import jax
import jax.numpy as jnp
from jax import lax
from jax.experimental import pallas as pl
from jax.experimental.pallas import tpu as pltpu
from jax.sharding import PartitionSpec as P

AXES = ("span", "tm")
PLANES = 128
WINDOW = 2 * PLANES
DEV = 128
TM = 32
SPAN_DEV = 4
R_LOC = 16
A_LOC = 96
HALF = A_LOC // 2
A_ALL = SPAN_DEV * A_LOC
B = 192
SEND1 = 64
SEND2 = 40
PITCH = R_LOC + 1
PITCH2 = 8 + 1
PARTS = 4
F32 = jnp.float32
BF16 = jnp.bfloat16
MIB = 1024 * 1024
VMEM = pl.BlockSpec(memory_space=pltpu.VMEM)
SMEM = pl.BlockSpec(memory_space=pltpu.SMEM)
HBM = pl.BlockSpec(memory_space=pltpu.HBM)


def lanes(shape):
    return lax.broadcasted_iota(jnp.int32, shape, len(shape) - 1)


def deal_kernel(start_ref, core_ref, time_ref, out_ref, held, window, turned, start, in_sem, time_sem, start_sem):
    order = (2, 0, 1)
    ins = {c: pltpu.make_async_copy(core_ref.at[c], held.at[c], in_sem.at[c]) for c in order}
    start_in = pltpu.make_async_copy(start_ref, start, start_sem)
    start_in.start()
    for c in order:
        ins[c].start()
    start_in.wait()
    base = jnp.minimum(start[0] // 128, (time_ref.shape[1] - WINDOW) // 128)
    window_in = pltpu.make_async_copy(
        time_ref.at[:, pl.ds(pl.multiple_of(base * 128, 128), WINDOW)], window, time_sem
    )
    window_in.start()
    eye = (
        lax.broadcasted_iota(jnp.int32, (B, B), 0) == lax.broadcasted_iota(jnp.int32, (B, B), 1)
    ).astype(BF16)
    main = lanes((1, 128)) < A_LOC
    gap = jnp.zeros((128 - A_LOC, B), BF16)
    for c in order:
        ins[c].wait()
        for r in range(0, R_LOC, 2):
            x = jnp.concatenate([held[c, r], gap, held[c, r + 1], gap], axis=0)
            y = lax.dot_general(eye, x, (((1,), (1,)), ((), ())), preferred_element_type=F32)
            turned.at[c][pl.ds(r, B, PITCH), :] = y[:, :128]
            turned.at[c][pl.ds(r + 1, B, PITCH), :] = y[:, 128:]
        if c == order[0]:
            window_in.wait()
            quarter = (A_LOC - 32 * lax.axis_index("span") + 128) % 128
            rows = pltpu.roll(window[...].astype(F32), (WINDOW - (start[0] - base * 128)) % WINDOW, 1)[:, :PLANES]
            rows = pltpu.roll(rows, quarter, 1)
        for i in range(48 if c < 2 else 32):
            device = 48 * c + i
            half = turned[2, pl.ds(PITCH * (128 + device // 2), R_LOC), :]
            side = (
                pltpu.roll(half, A_LOC - HALF * (device % 2), 1),
                pltpu.roll(half, A_LOC - 32 - HALF * (device % 2), 1),
                rows,
                None,
            )
            for q in range(4):
                block = turned[c, pl.ds(PITCH * (4 * i + q), R_LOC), :]
                if side[q] is not None:
                    block = jnp.where(main, block, side[q])
                out_ref[device, R_LOC * q : R_LOC * (q + 1), :] = block.astype(BF16)


def middle_kernel(owner_ref, held, span_0, span_1, span_2, span_3, out_ref, span, firsts):
    mine = lax.axis_index("span")
    owners = [owner_ref[j] for j in range(TM)]
    for k, part in enumerate((span_0, span_1, span_2, span_3)):
        base = lax.bitwise_xor(mine, k) * TM
        for j in range(TM):
            at = pl.multiple_of((base + owners[j]) * 8, 8)
            span[pl.ds(at, 8), :] = part[8 * j : 8 * (j + 1), :].astype(F32)
    lane3 = lanes((1, 1, 128))
    lane = lanes((1, 128))
    w = jnp.zeros((TM, R_LOC, 128), F32)
    for g in range(SPAN_DEV):
        piece = held[TM * g : TM * (g + 1), 2 * R_LOC : 3 * R_LOC, :].astype(F32)
        piece = pltpu.roll(piece, (32 * g - A_LOC) % 128, 2)
        w = jnp.where((lane3 >= 32 * g) & (lane3 < 32 * g + 32), piece, w)
    w = w.reshape(TM * R_LOC, 128).T.astype(BF16)
    low = HALF * lax.rem(lax.axis_index("tm"), 2)
    for g in range(SPAN_DEV):
        f = []
        for q in range(4):
            x = held[TM * g : TM * (g + 1), R_LOC * q : R_LOC * (q + 1), :].reshape(TM * R_LOC, 128)
            f.append(jnp.dot(w, x, preferred_element_type=F32))
            firsts[q, g] = f[q]
        half = jnp.where(lane < low + 32, pltpu.roll(f[0], low + 32, 1), pltpu.roll(f[1], low + 64, 1))
        firsts[4, g] = jnp.where((lane >= low) & (lane < low + HALF), half, 0.0)
    packed = []
    for q in range(5):
        f0, f1, f2, f3 = (firsts[q, g] for g in range(SPAN_DEV))
        tiles = (
            jnp.where(lane < 96, f0, pltpu.roll(f1, 96, 1)),
            jnp.where(lane < 64, pltpu.roll(f1, 96, 1), pltpu.roll(f2, 64, 1)),
            jnp.where(lane < 32, pltpu.roll(f2, 64, 1), pltpu.roll(f3, 32, 1)),
        )
        packed.append(jnp.concatenate(tiles, axis=1).astype(BF16))
    packed = jnp.concatenate(packed, axis=0)
    for g in range(SPAN_DEV):
        z = lax.dot_general(
            span[TM * 8 * g : TM * 8 * (g + 1)].astype(BF16),
            packed,
            (((1,), (1,)), ((), ())),
            preferred_element_type=F32,
        )
        for q in range(5):
            tile = z[:, 128 * q : 128 * (q + 1)].reshape(TM, 8, 128)
            out_ref[TM * g : TM * (g + 1), 8 * q : 8 * (q + 1), :] = tile.astype(BF16)


def height_kernel(held, height_ref, out_ref, height, wide, rows, stage, height_sem, out_sem):
    height_in = pltpu.make_async_copy(height_ref, height, height_sem)
    height_in.start()
    begins = (0, 48, 96)
    part = PLANES // PARTS
    outs = []
    for c in range(3):
        whole = B if c < 2 else 128
        for b in range(whole):
            source, q = begins[c] + b // 4, b % 4
            wide[c, pl.ds(PITCH2 * b, 8), :] = held[source, 8 * q : 8 * (q + 1), :].astype(F32)
        for b in range(whole, B):
            source = 2 * (b - 128)
            wide[c, pl.ds(PITCH2 * b, 8), :] = held[source, 32:, :].astype(F32) + held[source + 1, 32:, :].astype(F32)
        for s in range(8):
            x = wide.at[c][pl.ds(s, B, PITCH2), :].T
            rows.at[c, 0][pl.ds(s, PLANES, PITCH2), :] = x[:, :128]
            x = jnp.concatenate([x[:, 128:], jnp.zeros((PLANES, 256 - B), F32)], axis=1)
            rows.at[c, 1][pl.ds(s, PLANES, PITCH2), :] = x
        if c == 0:
            height_in.wait()
        for p in range(PARTS):
            x = [
                jnp.concatenate(
                    [rows[c, e, pl.ds(PITCH2 * t, 8), :] for t in range(part * p, part * (p + 1))], axis=0
                )
                for e in range(2)
            ]
            x = jnp.concatenate(x, axis=1)[:, :B].astype(BF16)
            y = jnp.dot(x, height[...], preferred_element_type=F32)
            at = pl.ds(part * p, part)
            stage[c, at] = y.reshape(part, 8, 512).astype(BF16)
            out = pltpu.make_async_copy(stage.at[c, at], out_ref.at[at, c], out_sem.at[PARTS * c + p])
            out.start()
            outs.append(out)
    for out in outs:
        out.wait()


def moves(step, flip):
    pairs = []
    for device in range(DEV):
        low, core, z, high, x = device // 64, device // 32 % 2, device // 8 % 4, device // 4 % 2, device % 4
        y = (2 * high + low + step) % 4
        pairs.append((device, ((y % 2 * 2 + (core ^ flip)) * 4 + z) * 8 + y // 2 * 4 + x))
    return pairs


def body(window_start, owner_map, core, span_factor, height_factor, time_factor):
    spans = [lax.ppermute(span_factor, AXES, moves(*way)) for way in ((-1, 1), (1, 0), (0, 1))]
    spans = [span_factor] + spans[::-1]
    sent = pl.pallas_call(
        deal_kernel,
        out_shape=pltpu.VMEM((DEV, SEND1, 128), BF16),
        in_specs=[HBM, HBM, HBM],
        out_specs=VMEM,
        scratch_shapes=[
            pltpu.VMEM((3, R_LOC, A_LOC, B), BF16),
            pltpu.VMEM((R_LOC, WINDOW), BF16),
            pltpu.VMEM((3, PITCH * B, 128), F32),
            pltpu.SMEM((1,), jnp.int32),
            pltpu.SemaphoreType.DMA((3,)),
            pltpu.SemaphoreType.DMA,
            pltpu.SemaphoreType.DMA,
        ],
        compiler_params=pltpu.CompilerParams(vmem_limit_bytes=60 * MIB),
        cost_estimate=pl.CostEstimate(flops=4_000_000_000, bytes_accessed=5_000_000, transcendentals=0),
        name="deal",
    )(window_start, core, time_factor.T)
    sent, *spans = lax.optimization_barrier((sent, *spans))
    got = lax.all_to_all(sent, AXES, 0, 0, tiled=True)
    sent = pl.pallas_call(
        middle_kernel,
        out_shape=jax.ShapeDtypeStruct((DEV, SEND2, 128), BF16),
        in_specs=[SMEM] + [VMEM] * 5,
        out_specs=VMEM,
        scratch_shapes=[
            pltpu.VMEM((8 * DEV, A_ALL), F32),
            pltpu.VMEM((5, SPAN_DEV, PLANES, 128), F32),
        ],
        compiler_params=pltpu.CompilerParams(vmem_limit_bytes=40 * MIB),
        name="middle",
    )(owner_map, got, *spans)
    got = lax.all_to_all(sent, AXES, 0, 0, tiled=True)
    return pl.pallas_call(
        height_kernel,
        out_shape=jax.ShapeDtypeStruct((PLANES, 3, 8, 512), BF16),
        in_specs=[VMEM, HBM],
        out_specs=HBM,
        scratch_shapes=[
            pltpu.VMEM((B, 512), BF16),
            pltpu.VMEM((3, PITCH2 * B, 128), F32),
            pltpu.VMEM((3, 2, PITCH2 * PLANES, 128), F32),
            pltpu.VMEM((3, PLANES, 8, 512), BF16),
            pltpu.SemaphoreType.DMA,
            pltpu.SemaphoreType.DMA((3 * PARTS,)),
        ],
        compiler_params=pltpu.CompilerParams(vmem_limit_bytes=40 * MIB),
        name="height",
    )(got, height_factor.T)


def solution(mesh):
    in_specs = (P(), P(), P(None, "tm", "span", None), P("span", None), P(), P(None, "tm"))
    out_specs = P(None, None, ("span", "tm"), None)
    return jax.shard_map(body, mesh=mesh, in_specs=in_specs, out_specs=out_specs, check_vma=False)
```

time: 86.5 us -> 81.1 us (0.938)
  starting transfers between devices: 11.5 us -> 4.27 us
  blocking collectives: 62.9 us -> 66.1 us
  Pallas kernels: 10.6 us -> 7.85 us
  waiting for transfers between devices: 0.53 us -> 1.97 us
    all_to_all x1 -> x2, blocking collectives: 30.3 us -> 66.1 us  [body(): got = lax.all_to_all(sent, AXES, 0, 0, tiled=True)]
    all_gather x1 -> x0, blocking collectives: 32.6 us -> none  [body(): span = lax.all_gather(tiles, 'span', axis=0, tiled=True)]
    all_to_all x1 -> x0, starting transfers between devices: 11.5 us -> none  [body(): got = lax.all_to_all(sent, AXES, 0, 0, tiled=True)]
    ppermute x0 -> x3, starting transfers between devices: none -> 4.27 us  [body(): lax.ppermute(span_factor, AXES, moves(*way))]
    pallas_call x1, Pallas kernels: 5.82 us -> 2.89 us  [body(): pl.pallas_call(deal_kernel, out_shape=pltpu.VMEM((DEV, SEND1, 128), BF16)...]
    ppermute x0 -> x3, waiting for transfers between devices: none -> 1.97 us  [body(): lax.ppermute(span_factor, AXES, moves(*way))]
  transfers between devices with their start and end apart: 1 -> 3, of which waited for: 1 -> 2; matrix products, arithmetic and copies ran while one was open for 0% -> 0% of each run, Pallas kernels for 0% -> 4%
where the time goes in v3:
time: 81.1 us; the launch traced here: 80.9 us
  blocking collectives  66.1 us (82%)
  Pallas kernels  7.85 us (10%)
  starting transfers between devices  4.27 us (5%)
  waiting for transfers between devices  1.97 us (2%)
    all_to_all x2, blocking collectives, body(): got = lax.all_to_all(sent, AXES, 0, 0, tiled=True)  66.1 us
    ppermute x3, starting transfers between devices, body(): lax.ppermute(span_factor, AXES, moves(*way))  4.27 us
    pallas_call x1, Pallas kernels, body(): pl.pallas_call(deal_kernel, out_shape=pltpu.VMEM((DEV, SEND1, 128), BF16)...  2.89 us
    pallas_call x1, Pallas kernels, body(): pl.pallas_call(height_kernel, out_shape=jax.ShapeDtypeStruct((PLANES, 3,...  2.48 us
    pallas_call x1, Pallas kernels, body(): pl.pallas_call(middle_kernel, out_shape=jax.ShapeDtypeStruct((DEV, SEND2,...  2.47 us
    ppermute x3, waiting for transfers between devices, body(): lax.ppermute(span_factor, AXES, moves(*way))  1.97 us
  transfers between devices with their start and end apart: 3, of which 2 were waited for; matrix products, arithmetic and copies ran while one was open for 0% of the time, Pallas kernels for 4%

profile of v3, /device:TPU:1, one launch (start us, length us, event | category | flops | bytes accessed | tf_op | source)
XLA Modules:
  0.0 80.9 jit_solution(4788572459961954936)
XLA Ops:
  0.0 2.1 %collective-permute-start.1 = (bf16[256,384]{1,0:T(8,128)(2,1)}, bf16[256,384]{1,0:T(8,128)(2,1)S(1)}, u32[]{:S(2)}, u32[]{:S(2)}) collective-permute-start(bf16[256,384]{1,0:T(8,128)(2,1)} %span_0), channel_id=1, source_target_pairs={{0,64},{1,65},{2,66},{3,67},{4,68},{5,69},{6,70},{7,71},{8,72},{9,... | collective-permute-start | bytes 589832 | tf_op jit(solution)/shard_map/ppermute | solution.py:178
  2.1 1.0 %collective-permute-start = (bf16[256,384]{1,0:T(8,128)(2,1)}, bf16[256,384]{1,0:T(8,128)(2,1)S(1)}, u32[]{:S(2)}, u32[]{:S(2)}) collective-permute-start(bf16[256,384]{1,0:T(8,128)(2,1)} %span_0), channel_id=1, source_target_pairs={{0,32},{1,33},{2,34},{3,35},{4,36},{5,37},{6,38},{7,39},{8,40},{9,... | collective-permute-start | bytes 589832 | tf_op jit(solution)/shard_map/ppermute | solution.py:178
  3.1 1.2 %collective-permute-start.2 = (bf16[256,384]{1,0:T(8,128)(2,1)}, bf16[256,384]{1,0:T(8,128)(2,1)S(1)}, u32[]{:S(2)}, u32[]{:S(2)}) collective-permute-start(bf16[256,384]{1,0:T(8,128)(2,1)} %span_0), channel_id=1, source_target_pairs={{0,100},{1,101},{2,102},{3,103},{4,96},{5,97},{6,98},{7,99},{8,108... | collective-permute-start | bytes 589832 | tf_op jit(solution)/shard_map/ppermute | solution.py:178
  4.9 2.9 %deal.1 = bf16[128,64,128]{2,1,0:T(8,128)(2,1)S(1)} custom-call(s32[1]{0:T(128)S(6)} %copy.7.start_ref, bf16[3,16,96,192]{3,2,1,0:T(8,128)(2,1)} %core_ref.1, bf16[16,4096]{1,0:T(8,128)(2,1)} %bitcast.3), custom_call_target="tpu_custom_call" | custom-call | flops 4000000000 | bytes 5000000 | tf_op jit(solution)/shard_map/deal/pallas_call | solution.py:180
  7.8 0.0 copy-start
  7.8 0.0 copy-start.2
  7.8 0.4 collective-permute-done.1.span_2
  8.2 0.0 collective-permute-done.span_1
  8.2 1.6 %collective-permute-done.2.span_3 = bf16[256,384]{1,0:T(8,128)(2,1)S(1)} collective-permute-done((bf16[256,384]{1,0:T(8,128)(2,1)}, bf16[256,384]{1,0:T(8,128)(2,1)S(1)}, u32[]{:S(2)}, u32[]{:S(2)}) %collective-permute-start.2) | collective-permute-done | bytes 196640 | tf_op jit(solution)/shard_map/ppermute | solution.py:178
  9.8 39.9 %all_to_all.10.held = bf16[128,64,128]{2,1,0:T(8,128)(2,1)S(1)} all-to-all(bf16[128,64,128]{2,1,0:T(8,128)(2,1)S(1)} %deal.1), channel_id=1, replica_groups=mesh['span'=4,'tm'=32] {'span','tm'}, dimensions={0} | all-to-all | bytes 4194304 | tf_op jit(solution)/shard_map/all_to_all | solution.py:199
  49.7 0.0 copy-done
  49.7 0.0 copy-done.2
  49.7 2.5 %middle.1 = bf16[128,40,128]{2,1,0:T(8,128)(2,1)S(1)} custom-call(s32[32]{0:T(128)S(1)} %copy-done.2, bf16[128,64,128]{2,1,0:T(8,128)(2,1)S(1)} %all_to_all.10.held, bf16[256,384]{1,0:T(8,128)(2,1)S(1)} %copy-done, bf16[256,384]{1,0:T(8,128)(2,1)S(1)} %collective-permute-done.span_1, bf16[256,384]{1,0:T(8,128)(2,1)S(1)} %collective-permute-done.1.span_2, ...), custom_call_target="tpu_custom_call" | custom-call | tf_op jit(solution)/shard_map/middle/pallas_call | solution.py:200
  52.2 0.0 copy-start.1
  52.2 26.2 %all_to_all.11.held = bf16[128,40,128]{2,1,0:T(8,128)(2,1)S(1)} all-to-all(bf16[128,40,128]{2,1,0:T(8,128)(2,1)S(1)} %middle.1), channel_id=1, replica_groups=mesh['span'=4,'tm'=32] {'span','tm'}, dimensions={0} | all-to-all | bytes 2621440 | tf_op jit(solution)/shard_map/all_to_all | solution.py:212
  78.4 0.0 copy-done.1
  78.4 2.5 %height.1 = bf16[128,3,8,512]{3,2,1,0:T(8,128)(2,1)} custom-call(bf16[128,40,128]{2,1,0:T(8,128)(2,1)S(1)} %all_to_all.11.held, bf16[192,512]{1,0:T(8,128)(2,1)S(1)} %bitcast.2), custom_call_target="tpu_custom_call" | custom-call | tf_op jit(solution)/shard_map/height/pallas_call | solution.py:213
Async XLA Ops:
  0.0 8.2 %collective-permute-start.1 = (bf16[256,384]{1,0:T(8,128)(2,1)}, bf16[256,384]{1,0:T(8,128)(2,1)S(1)}, u32[]{:S(2)}, u32[]{:S(2)}) collective-permute-start(bf16[256,384]{1,0:T(8,128)(2,1)} %span_0), channel_id=1, source_target_pairs={{0,64},{1,65},{2,66},{3,67},{4,68},{5,69},{6,70},{7,71},{8,72},{9,... | collective-permute-start | bytes 589832 | tf_op jit(solution)/shard_map/ppermute | solution.py:178
  2.1 6.1 %collective-permute-start = (bf16[256,384]{1,0:T(8,128)(2,1)}, bf16[256,384]{1,0:T(8,128)(2,1)S(1)}, u32[]{:S(2)}, u32[]{:S(2)}) collective-permute-start(bf16[256,384]{1,0:T(8,128)(2,1)} %span_0), channel_id=1, source_target_pairs={{0,32},{1,33},{2,34},{3,35},{4,36},{5,37},{6,38},{7,39},{8,40},{9,... | collective-permute-start | bytes 589832 | tf_op jit(solution)/shard_map/ppermute | solution.py:178
  3.1 6.7 %collective-permute-start.2 = (bf16[256,384]{1,0:T(8,128)(2,1)}, bf16[256,384]{1,0:T(8,128)(2,1)S(1)}, u32[]{:S(2)}, u32[]{:S(2)}) collective-permute-start(bf16[256,384]{1,0:T(8,128)(2,1)} %span_0), channel_id=1, source_target_pairs={{0,100},{1,101},{2,102},{3,103},{4,96},{5,97},{6,98},{7,99},{8,108... | collective-permute-start | bytes 589832 | tf_op jit(solution)/shard_map/ppermute | solution.py:178
  7.8 41.9 %copy-start = (bf16[256,384]{1,0:T(8,128)(2,1)S(1)}, bf16[256,384]{1,0:T(8,128)(2,1)}, u32[]{:S(2)}) copy-start(bf16[256,384]{1,0:T(8,128)(2,1)} %span_0) | copy-start | bytes 589828
  7.8 41.9 %copy-start.2 = (s32[32]{0:T(128)S(1)}, s32[32]{0:T(128)}, u32[]{:S(2)}) copy-start(s32[32]{0:T(128)} %owner_ref.1) | copy-start | bytes 388
  52.2 26.2 %copy-start.1 = (bf16[512,192]{0,1:T(8,128)(2,1)S(1)}, bf16[512,192]{0,1:T(8,128)(2,1)}, u32[]{:S(2)}) copy-start(bf16[512,192]{0,1:T(8,128)(2,1)} %param.10) | copy-start | bytes 589828

commit v4 on v3

--- a/solution.py
+++ b/solution.py
@@ -33,7 +33,9 @@
     return lax.broadcasted_iota(jnp.int32, shape, len(shape) - 1)
 
 
-def deal_kernel(start_ref, core_ref, time_ref, out_ref, held, window, turned, start, in_sem, time_sem, start_sem):
+def deal_kernel(
+    start_ref, core_ref, time_ref, out_ref, held, window, turned, stage, start, in_sem, time_sem, start_sem, out_sem
+):
     order = (2, 0, 1)
     ins = {c: pltpu.make_async_copy(core_ref.at[c], held.at[c], in_sem.at[c]) for c in order}
     start_in = pltpu.make_async_copy(start_ref, start, start_sem)
@@ -51,6 +53,7 @@
     ).astype(BF16)
     main = lanes((1, 128)) < A_LOC
     gap = jnp.zeros((128 - A_LOC, B), BF16)
+    outs = []
     for c in order:
         ins[c].wait()
         for r in range(0, R_LOC, 2):
@@ -76,7 +79,12 @@
                 block = turned[c, pl.ds(PITCH * (4 * i + q), R_LOC), :]
                 if side[q] is not None:
                     block = jnp.where(main, block, side[q])
-                out_ref[device, R_LOC * q : R_LOC * (q + 1), :] = block.astype(BF16)
+                stage[device, R_LOC * q : R_LOC * (q + 1), :] = block.astype(BF16)
+        at = pl.ds(48 * c, 48 if c < 2 else 32)
+        outs.append(pltpu.make_async_copy(stage.at[at], out_ref.at[at], out_sem.at[c]))
+        outs[-1].start()
+    for out in outs:
+        out.wait()
 
 
 def middle_kernel(owner_ref, held, span_0, span_1, span_2, span_3, out_ref, span, firsts):
@@ -98,9 +106,14 @@
     low = HALF * lax.rem(lax.axis_index("tm"), 2)
     for g in range(SPAN_DEV):
         f = []
+        for q in (0, 2):
+            x = [
+                held[TM * g : TM * (g + 1), R_LOC * p : R_LOC * (p + 1), :].reshape(TM * R_LOC, 128)
+                for p in (q, q + 1)
+            ]
+            y = jnp.dot(w, jnp.concatenate(x, axis=1), preferred_element_type=F32)
+            f += [y[:, :128], y[:, 128:]]
         for q in range(4):
-            x = held[TM * g : TM * (g + 1), R_LOC * q : R_LOC * (q + 1), :].reshape(TM * R_LOC, 128)
-            f.append(jnp.dot(w, x, preferred_element_type=F32))
             firsts[q, g] = f[q]
         half = jnp.where(lane < low + 32, pltpu.roll(f[0], low + 32, 1), pltpu.roll(f[1], low + 64, 1))
         firsts[4, g] = jnp.where((lane >= low) & (lane < low + HALF), half, 0.0)
@@ -114,16 +127,11 @@
         )
         packed.append(jnp.concatenate(tiles, axis=1).astype(BF16))
     packed = jnp.concatenate(packed, axis=0)
-    for g in range(SPAN_DEV):
-        z = lax.dot_general(
-            span[TM * 8 * g : TM * 8 * (g + 1)].astype(BF16),
-            packed,
-            (((1,), (1,)), ((), ())),
-            preferred_element_type=F32,
-        )
-        for q in range(5):
-            tile = z[:, 128 * q : 128 * (q + 1)].reshape(TM, 8, 128)
-            out_ref[TM * g : TM * (g + 1), 8 * q : 8 * (q + 1), :] = tile.astype(BF16)
+    z = lax.dot_general(
+        span[...].astype(BF16), packed, (((1,), (1,)), ((), ())), preferred_element_type=F32
+    )
+    for q in range(5):
+        out_ref[:, 8 * q : 8 * (q + 1), :] = z[:, 128 * q : 128 * (q + 1)].reshape(DEV, 8, 128).astype(BF16)
 
 
 def height_kernel(held, height_ref, out_ref, height, wide, rows, stage, height_sem, out_sem):
@@ -175,27 +183,29 @@
 
 
 def body(window_start, owner_map, core, span_factor, height_factor, time_factor):
-    spans = [lax.ppermute(span_factor, AXES, moves(*way)) for way in ((-1, 1), (1, 0), (0, 1))]
-    spans = [span_factor] + spans[::-1]
+    across = lax.ppermute(span_factor, AXES, moves(1, 0))
     sent = pl.pallas_call(
         deal_kernel,
-        out_shape=pltpu.VMEM((DEV, SEND1, 128), BF16),
+        out_shape=jax.ShapeDtypeStruct((DEV, SEND1, 128), BF16),
         in_specs=[HBM, HBM, HBM],
-        out_specs=VMEM,
+        out_specs=HBM,
         scratch_shapes=[
             pltpu.VMEM((3, R_LOC, A_LOC, B), BF16),
             pltpu.VMEM((R_LOC, WINDOW), BF16),
             pltpu.VMEM((3, PITCH * B, 128), F32),
+            pltpu.VMEM((DEV, SEND1, 128), BF16),
             pltpu.SMEM((1,), jnp.int32),
             pltpu.SemaphoreType.DMA((3,)),
             pltpu.SemaphoreType.DMA,
             pltpu.SemaphoreType.DMA,
+            pltpu.SemaphoreType.DMA((3,)),
         ],
         compiler_params=pltpu.CompilerParams(vmem_limit_bytes=60 * MIB),
         cost_estimate=pl.CostEstimate(flops=4_000_000_000, bytes_accessed=5_000_000, transcendentals=0),
         name="deal",
     )(window_start, core, time_factor.T)
-    sent, *spans = lax.optimization_barrier((sent, *spans))
+    sent, span_factor, across = lax.optimization_barrier((sent, span_factor, across))
+    spans = [span_factor, lax.ppermute(span_factor, AXES, moves(0, 1)), across, lax.ppermute(across, AXES, moves(0, 1))]
     got = lax.all_to_all(sent, AXES, 0, 0, tiled=True)
     sent = pl.pallas_call(
         middle_kernel,

time: 81.1 us -> 79.8 us (0.984)
  blocking collectives: 66.1 us -> 26.2 us
  waiting for transfers between devices: 1.97 us -> 30.7 us
  starting transfers between devices: 4.27 us -> 13.5 us
    all_to_all x2 -> x1, blocking collectives: 66.1 us -> 26.2 us  [body(): got = lax.all_to_all(sent, AXES, 0, 0, tiled=True)]
    all_to_all x0 -> x1, waiting for transfers between devices: none -> 27.7 us  [body(): got = lax.all_to_all(sent, AXES, 0, 0, tiled=True)]
    all_to_all x0 -> x1, starting transfers between devices: none -> 10.1 us  [body(): got = lax.all_to_all(sent, AXES, 0, 0, tiled=True)]
    ppermute x3, waiting for transfers between devices: 1.97 us -> 2.99 us  [the longest x1 1.64 us: body(): across = lax.ppermute(span_factor, AXES, moves(1, 0))]
    pallas_call x1, Pallas kernels: 2.89 us -> 3.79 us  [body(): pl.pallas_call(deal_kernel, out_shape=jax.ShapeDtypeStruct((DEV, SEND1, 1...]
    ppermute x3, starting transfers between devices: 4.27 us -> 3.37 us  [the longest x1 2.13 us: body(): across = lax.ppermute(span_factor, AXES, moves(1, 0))]
  transfers between devices with their start and end apart: 3 -> 4, of which waited for: 2 -> 4; matrix products, arithmetic and copies ran while one was open for 0% -> 0% of each run, Pallas kernels for 4% -> 5%
where the time goes in v4:
time: 79.8 us; the launch traced here: 79.5 us
  waiting for transfers between devices  30.7 us (38%)
  blocking collectives  26.2 us (33%)
  starting transfers between devices  13.5 us (17%)
  Pallas kernels  8.49 us (11%)
    all_to_all x1, waiting for transfers between devices, body(): got = lax.all_to_all(sent, AXES, 0, 0, tiled=True)  27.7 us
    all_to_all x1, blocking collectives, body(): got = lax.all_to_all(sent, AXES, 0, 0, tiled=True)  26.2 us
    all_to_all x1, starting transfers between devices, body(): got = lax.all_to_all(sent, AXES, 0, 0, tiled=True)  10.1 us
    pallas_call x1, Pallas kernels, body(): pl.pallas_call(deal_kernel, out_shape=jax.ShapeDtypeStruct((DEV, SEND1, 1...  3.79 us
    pallas_call x1, Pallas kernels, body(): pl.pallas_call(height_kernel, out_shape=jax.ShapeDtypeStruct((PLANES, 3,...  2.49 us
    pallas_call x1, Pallas kernels, body(): pl.pallas_call(middle_kernel, out_shape=jax.ShapeDtypeStruct((DEV, SEND2,...  2.2 us
    ppermute x1, starting transfers between devices, body(): across = lax.ppermute(span_factor, AXES, moves(1, 0))  2.13 us
    ppermute x1, waiting for transfers between devices, body(): across = lax.ppermute(span_factor, AXES, moves(1, 0))  1.64 us
  transfers between devices with their start and end apart: 4, of which 4 were waited for; matrix products, arithmetic and copies ran while one was open for 0% of the time, Pallas kernels for 5%

profile of v4, /device:TPU:1, one launch (start us, length us, event | category | flops | bytes accessed | tf_op | source)
XLA Modules:
  0.0 79.5 jit_solution(14677174108824872755)
XLA Ops:
  0.0 2.1 %collective-permute-start = (bf16[256,384]{1,0:T(8,128)(2,1)}, bf16[256,384]{1,0:T(8,128)(2,1)S(1)}, u32[]{:S(2)}, u32[]{:S(2)}) collective-permute-start(bf16[256,384]{1,0:T(8,128)(2,1)} %span_0), channel_id=1, source_target_pairs={{0,64},{1,65},{2,66},{3,67},{4,68},{5,69},{6,70},{7,71},{8,72},{9,... | collective-permute-start | bytes 589832 | tf_op jit(solution)/shard_map/ppermute | solution.py:186
  2.8 3.8 %deal.1 = bf16[128,64,128]{2,1,0:T(8,128)(2,1)} custom-call(s32[1]{0:T(128)S(6)} %copy.7.start_ref, bf16[3,16,96,192]{3,2,1,0:T(8,128)(2,1)} %core_ref.1, bf16[16,4096]{1,0:T(8,128)(2,1)} %bitcast.3), custom_call_target="tpu_custom_call" | custom-call | flops 4000000000 | bytes 5000000 | tf_op jit(solution)/shard_map/deal/pallas_call | solution.py:187
  6.6 0.0 copy-start
  6.6 0.0 copy-start.2
  6.6 1.6 %collective-permute-done.span_2 = bf16[256,384]{1,0:T(8,128)(2,1)S(1)} collective-permute-done((bf16[256,384]{1,0:T(8,128)(2,1)}, bf16[256,384]{1,0:T(8,128)(2,1)S(1)}, u32[]{:S(2)}, u32[]{:S(2)}) %collective-permute-start) | collective-permute-done | bytes 196640 | tf_op jit(solution)/shard_map/ppermute | solution.py:186
  8.2 10.1 %all-to-all-start = ((bf16[128,64,128]{2,1,0:T(8,128)(2,1)}), bf16[128,64,128]{2,1,0:T(8,128)(2,1)S(1)}, u32[]{:S(2)}, u32[]{:S(2)}) async-start(bf16[128,64,128]{2,1,0:T(8,128)(2,1)} %deal.1), calls=%async_computation | async-start | bytes 4194304 | tf_op jit(solution)/shard_map/all_to_all | solution.py:209
  18.4 0.0 copy-done
  18.4 1.1 %collective-permute-start.1 = (bf16[256,384]{1,0:T(8,128)(2,1)S(1)}, bf16[256,384]{1,0:T(8,128)(2,1)S(1)}, u32[]{:S(2)}, u32[]{:S(2)}) collective-permute-start(bf16[256,384]{1,0:T(8,128)(2,1)S(1)} %copy-done), channel_id=1, source_target_pairs={{0,32},{1,33},{2,34},{3,35},{4,36},{5,37},{6,38},{7,39},{8,40},{9,... | collective-permute-start | bytes 589832 | tf_op jit(solution)/shard_map/ppermute | solution.py:208
  19.5 0.1 collective-permute-start.2
  19.6 1.0 %collective-permute-done.1.span_1 = bf16[256,384]{1,0:T(8,128)(2,1)S(1)} collective-permute-done((bf16[256,384]{1,0:T(8,128)(2,1)S(1)}, bf16[256,384]{1,0:T(8,128)(2,1)S(1)}, u32[]{:S(2)}, u32[]{:S(2)}) %collective-permute-start.1) | collective-permute-done | bytes 196640 | tf_op jit(solution)/shard_map/ppermute | solution.py:208
  20.6 0.4 collective-permute-done.2.span_3
  21.0 27.7 %all-to-all-done.held = bf16[128,64,128]{2,1,0:T(8,128)(2,1)S(1)} async-done(((bf16[128,64,128]{2,1,0:T(8,128)(2,1)}), bf16[128,64,128]{2,1,0:T(8,128)(2,1)S(1)}, u32[]{:S(2)}, u32[]{:S(2)}) %all-to-all-start) | async-done | bytes 2097184 | tf_op jit(solution)/shard_map/all_to_all | solution.py:209
  48.7 0.0 copy-done.2
  48.7 2.2 %middle.1 = bf16[128,40,128]{2,1,0:T(8,128)(2,1)S(1)} custom-call(s32[32]{0:T(128)S(1)} %copy-done.2, bf16[128,64,128]{2,1,0:T(8,128)(2,1)S(1)} %all-to-all-done.held, bf16[256,384]{1,0:T(8,128)(2,1)S(1)} %copy-done, bf16[256,384]{1,0:T(8,128)(2,1)S(1)} %collective-permute-done.1.span_1, bf16[256,384]{1,0:T(8,128)(2,1)S(1)} %collective-permute-done.span_2, ...), custom_call_target="tpu_custom_call" | custom-call | tf_op jit(solution)/shard_map/middle/pallas_call | solution.py:210
  50.9 0.0 copy-start.1
  50.9 26.2 %all_to_all.10.held = bf16[128,40,128]{2,1,0:T(8,128)(2,1)S(1)} all-to-all(bf16[128,40,128]{2,1,0:T(8,128)(2,1)S(1)} %middle.1), channel_id=1, replica_groups=mesh['span'=4,'tm'=32] {'span','tm'}, dimensions={0} | all-to-all | bytes 2621440 | tf_op jit(solution)/shard_map/all_to_all | solution.py:222
  77.1 0.0 copy-done.1
  77.1 2.5 %height.1 = bf16[128,3,8,512]{3,2,1,0:T(8,128)(2,1)} custom-call(bf16[128,40,128]{2,1,0:T(8,128)(2,1)S(1)} %all_to_all.10.held, bf16[192,512]{1,0:T(8,128)(2,1)S(1)} %bitcast.2), custom_call_target="tpu_custom_call" | custom-call | tf_op jit(solution)/shard_map/height/pallas_call | solution.py:223
Async XLA Ops:
  0.0 8.2 %collective-permute-start = (bf16[256,384]{1,0:T(8,128)(2,1)}, bf16[256,384]{1,0:T(8,128)(2,1)S(1)}, u32[]{:S(2)}, u32[]{:S(2)}) collective-permute-start(bf16[256,384]{1,0:T(8,128)(2,1)} %span_0), channel_id=1, source_target_pairs={{0,64},{1,65},{2,66},{3,67},{4,68},{5,69},{6,70},{7,71},{8,72},{9,... | collective-permute-start | bytes 589832 | tf_op jit(solution)/shard_map/ppermute | solution.py:186
  6.6 11.8 %copy-start = (bf16[256,384]{1,0:T(8,128)(2,1)S(1)}, bf16[256,384]{1,0:T(8,128)(2,1)}, u32[]{:S(2)}) copy-start(bf16[256,384]{1,0:T(8,128)(2,1)} %span_0) | copy-start | bytes 589828
  6.6 42.1 %copy-start.2 = (s32[32]{0:T(128)S(1)}, s32[32]{0:T(128)}, u32[]{:S(2)}) copy-start(s32[32]{0:T(128)} %owner_ref.1) | copy-start | bytes 388
  8.2 40.4 %all-to-all-start = ((bf16[128,64,128]{2,1,0:T(8,128)(2,1)}), bf16[128,64,128]{2,1,0:T(8,128)(2,1)S(1)}, u32[]{:S(2)}, u32[]{:S(2)}) async-start(bf16[128,64,128]{2,1,0:T(8,128)(2,1)} %deal.1), calls=%async_computation | async-start | bytes 4194304 | tf_op jit(solution)/shard_map/all_to_all | solution.py:209
  18.4 2.2 %collective-permute-start.1 = (bf16[256,384]{1,0:T(8,128)(2,1)S(1)}, bf16[256,384]{1,0:T(8,128)(2,1)S(1)}, u32[]{:S(2)}, u32[]{:S(2)}) collective-permute-start(bf16[256,384]{1,0:T(8,128)(2,1)S(1)} %copy-done), channel_id=1, source_target_pairs={{0,32},{1,33},{2,34},{3,35},{4,36},{5,37},{6,38},{7,39},{8,40},{9,... | collective-permute-start | bytes 589832 | tf_op jit(solution)/shard_map/ppermute | solution.py:208
  19.5 1.4 %collective-permute-start.2 = (bf16[256,384]{1,0:T(8,128)(2,1)S(1)}, bf16[256,384]{1,0:T(8,128)(2,1)S(1)}, u32[]{:S(2)}, u32[]{:S(2)}) collective-permute-start(bf16[256,384]{1,0:T(8,128)(2,1)S(1)} %collective-permute-done.span_2), channel_id=1, source_target_pairs={{0,32},{1,33},{2,34},{3,35},{4,36},{5,37},{6,38},{7,39},{8,40},{9,... | collective-permute-start | bytes 589832 | tf_op jit(solution)/shard_map/ppermute | solution.py:208
  50.9 26.2 %copy-start.1 = (bf16[512,192]{0,1:T(8,128)(2,1)S(1)}, bf16[512,192]{0,1:T(8,128)(2,1)}, u32[]{:S(2)}) copy-start(bf16[512,192]{0,1:T(8,128)(2,1)} %param.10) | copy-start | bytes 589828

commit v5 on v4

--- a/solution.py
+++ b/solution.py
@@ -177,7 +177,7 @@
     pairs = []
     for device in range(DEV):
         low, core, z, high, x = device // 64, device // 32 % 2, device // 8 % 4, device // 4 % 2, device % 4
-        y = (2 * high + low + step) % 4
+        y = (2 * high + low + (-step if core else step)) % 4
         pairs.append((device, ((y % 2 * 2 + (core ^ flip)) * 4 + z) * 8 + y // 2 * 4 + x))
     return pairs
 

time: 79.8 us -> 78.8 us (0.987)
  waiting for transfers between devices: 30.7 us -> 29.1 us
    ppermute x1, waiting for transfers between devices: 1.64 us -> 0.01 us  [body(): across = lax.ppermute(span_factor, AXES, moves(1, 0))]
    ppermute x1, starting transfers between devices: 2.13 us -> 3.56 us  [body(): across = lax.ppermute(span_factor, AXES, moves(1, 0))]
  transfers between devices with their start and end apart: 4 -> 4, of which waited for: 4 -> 3; matrix products, arithmetic and copies ran while one was open for 0% -> 0% of each run, Pallas kernels for 5% -> 5%
where the time goes in v5:
time: 78.8 us; the launch traced here: 78.6 us
  waiting for transfers between devices  29.1 us (37%)
  blocking collectives  26.2 us (33%)
  starting transfers between devices  14.1 us (18%)
  Pallas kernels  8.48 us (11%)
    all_to_all x1, waiting for transfers between devices, body(): got = lax.all_to_all(sent, AXES, 0, 0, tiled=True)  27.7 us
    all_to_all x1, blocking collectives, body(): got = lax.all_to_all(sent, AXES, 0, 0, tiled=True)  26.2 us
    all_to_all x1, starting transfers between devices, body(): got = lax.all_to_all(sent, AXES, 0, 0, tiled=True)  9.34 us
    pallas_call x1, Pallas kernels, body(): pl.pallas_call(deal_kernel, out_shape=jax.ShapeDtypeStruct((DEV, SEND1, 1...  3.78 us
    ppermute x1, starting transfers between devices, body(): across = lax.ppermute(span_factor, AXES, moves(1, 0))  3.56 us
    pallas_call x1, Pallas kernels, body(): pl.pallas_call(height_kernel, out_shape=jax.ShapeDtypeStruct((PLANES, 3,...  2.5 us
    pallas_call x1, Pallas kernels, body(): pl.pallas_call(middle_kernel, out_shape=jax.ShapeDtypeStruct((DEV, SEND2,...  2.2 us
  transfers between devices with their start and end apart: 4, of which 3 were waited for; matrix products, arithmetic and copies ran while one was open for 0% of the time, Pallas kernels for 5%

profile of v5, /device:TPU:1, one launch (start us, length us, event | category | flops | bytes accessed | tf_op | source)
XLA Modules:
  0.0 78.6 jit_solution(6314761704875715476)
XLA Ops:
  0.0 3.6 %collective-permute-start = (bf16[256,384]{1,0:T(8,128)(2,1)}, bf16[256,384]{1,0:T(8,128)(2,1)S(1)}, u32[]{:S(2)}, u32[]{:S(2)}) collective-permute-start(bf16[256,384]{1,0:T(8,128)(2,1)} %span_0), channel_id=1, source_target_pairs={{0,64},{1,65},{2,66},{3,67},{4,68},{5,69},{6,70},{7,71},{8,72},{9,... | collective-permute-start | bytes 589832 | tf_op jit(solution)/shard_map/ppermute | solution.py:186
  4.2 3.8 %deal.1 = bf16[128,64,128]{2,1,0:T(8,128)(2,1)} custom-call(s32[1]{0:T(128)S(6)} %copy.7.start_ref, bf16[3,16,96,192]{3,2,1,0:T(8,128)(2,1)} %core_ref.1, bf16[16,4096]{1,0:T(8,128)(2,1)} %bitcast.3), custom_call_target="tpu_custom_call" | custom-call | flops 4000000000 | bytes 5000000 | tf_op jit(solution)/shard_map/deal/pallas_call | solution.py:187
  8.0 0.0 copy-start
  8.0 0.0 copy-start.2
  8.0 0.0 collective-permute-done.span_2
  8.0 9.3 %all-to-all-start = ((bf16[128,64,128]{2,1,0:T(8,128)(2,1)}), bf16[128,64,128]{2,1,0:T(8,128)(2,1)S(1)}, u32[]{:S(2)}, u32[]{:S(2)}) async-start(bf16[128,64,128]{2,1,0:T(8,128)(2,1)} %deal.1), calls=%async_computation | async-start | bytes 4194304 | tf_op jit(solution)/shard_map/all_to_all | solution.py:209
  17.4 0.0 copy-done
  17.4 1.1 %collective-permute-start.1 = (bf16[256,384]{1,0:T(8,128)(2,1)S(1)}, bf16[256,384]{1,0:T(8,128)(2,1)S(1)}, u32[]{:S(2)}, u32[]{:S(2)}) collective-permute-start(bf16[256,384]{1,0:T(8,128)(2,1)S(1)} %copy-done), channel_id=1, source_target_pairs={{0,32},{1,33},{2,34},{3,35},{4,36},{5,37},{6,38},{7,39},{8,40},{9,... | collective-permute-start | bytes 589832 | tf_op jit(solution)/shard_map/ppermute | solution.py:208
  18.5 0.1 collective-permute-start.2
  18.6 1.0 %collective-permute-done.1.span_1 = bf16[256,384]{1,0:T(8,128)(2,1)S(1)} collective-permute-done((bf16[256,384]{1,0:T(8,128)(2,1)S(1)}, bf16[256,384]{1,0:T(8,128)(2,1)S(1)}, u32[]{:S(2)}, u32[]{:S(2)}) %collective-permute-start.1) | collective-permute-done | bytes 196640 | tf_op jit(solution)/shard_map/ppermute | solution.py:208
  19.6 0.4 collective-permute-done.2.span_3
  20.0 27.7 %all-to-all-done.held = bf16[128,64,128]{2,1,0:T(8,128)(2,1)S(1)} async-done(((bf16[128,64,128]{2,1,0:T(8,128)(2,1)}), bf16[128,64,128]{2,1,0:T(8,128)(2,1)S(1)}, u32[]{:S(2)}, u32[]{:S(2)}) %all-to-all-start) | async-done | bytes 2097184 | tf_op jit(solution)/shard_map/all_to_all | solution.py:209
  47.7 0.0 copy-done.2
  47.7 2.2 %middle.1 = bf16[128,40,128]{2,1,0:T(8,128)(2,1)S(1)} custom-call(s32[32]{0:T(128)S(1)} %copy-done.2, bf16[128,64,128]{2,1,0:T(8,128)(2,1)S(1)} %all-to-all-done.held, bf16[256,384]{1,0:T(8,128)(2,1)S(1)} %copy-done, bf16[256,384]{1,0:T(8,128)(2,1)S(1)} %collective-permute-done.1.span_1, bf16[256,384]{1,0:T(8,128)(2,1)S(1)} %collective-permute-done.span_2, ...), custom_call_target="tpu_custom_call" | custom-call | tf_op jit(solution)/shard_map/middle/pallas_call | solution.py:210
  49.9 0.0 copy-start.1
  49.9 26.2 %all_to_all.10.held = bf16[128,40,128]{2,1,0:T(8,128)(2,1)S(1)} all-to-all(bf16[128,40,128]{2,1,0:T(8,128)(2,1)S(1)} %middle.1), channel_id=1, replica_groups=mesh['span'=4,'tm'=32] {'span','tm'}, dimensions={0} | all-to-all | bytes 2621440 | tf_op jit(solution)/shard_map/all_to_all | solution.py:222
  76.1 0.0 copy-done.1
  76.1 2.5 %height.1 = bf16[128,3,8,512]{3,2,1,0:T(8,128)(2,1)} custom-call(bf16[128,40,128]{2,1,0:T(8,128)(2,1)S(1)} %all_to_all.10.held, bf16[192,512]{1,0:T(8,128)(2,1)S(1)} %bitcast.2), custom_call_target="tpu_custom_call" | custom-call | tf_op jit(solution)/shard_map/height/pallas_call | solution.py:223
Async XLA Ops:
  0.0 8.0 %collective-permute-start = (bf16[256,384]{1,0:T(8,128)(2,1)}, bf16[256,384]{1,0:T(8,128)(2,1)S(1)}, u32[]{:S(2)}, u32[]{:S(2)}) collective-permute-start(bf16[256,384]{1,0:T(8,128)(2,1)} %span_0), channel_id=1, source_target_pairs={{0,64},{1,65},{2,66},{3,67},{4,68},{5,69},{6,70},{7,71},{8,72},{9,... | collective-permute-start | bytes 589832 | tf_op jit(solution)/shard_map/ppermute | solution.py:186
  8.0 9.4 %copy-start = (bf16[256,384]{1,0:T(8,128)(2,1)S(1)}, bf16[256,384]{1,0:T(8,128)(2,1)}, u32[]{:S(2)}) copy-start(bf16[256,384]{1,0:T(8,128)(2,1)} %span_0) | copy-start | bytes 589828
  8.0 39.7 %copy-start.2 = (s32[32]{0:T(128)S(1)}, s32[32]{0:T(128)}, u32[]{:S(2)}) copy-start(s32[32]{0:T(128)} %owner_ref.1) | copy-start | bytes 388
  8.0 39.7 %all-to-all-start = ((bf16[128,64,128]{2,1,0:T(8,128)(2,1)}), bf16[128,64,128]{2,1,0:T(8,128)(2,1)S(1)}, u32[]{:S(2)}, u32[]{:S(2)}) async-start(bf16[128,64,128]{2,1,0:T(8,128)(2,1)} %deal.1), calls=%async_computation | async-start | bytes 4194304 | tf_op jit(solution)/shard_map/all_to_all | solution.py:209
  17.4 2.2 %collective-permute-start.1 = (bf16[256,384]{1,0:T(8,128)(2,1)S(1)}, bf16[256,384]{1,0:T(8,128)(2,1)S(1)}, u32[]{:S(2)}, u32[]{:S(2)}) collective-permute-start(bf16[256,384]{1,0:T(8,128)(2,1)S(1)} %copy-done), channel_id=1, source_target_pairs={{0,32},{1,33},{2,34},{3,35},{4,36},{5,37},{6,38},{7,39},{8,40},{9,... | collective-permute-start | bytes 589832 | tf_op jit(solution)/shard_map/ppermute | solution.py:208
  18.5 1.4 %collective-permute-start.2 = (bf16[256,384]{1,0:T(8,128)(2,1)S(1)}, bf16[256,384]{1,0:T(8,128)(2,1)S(1)}, u32[]{:S(2)}, u32[]{:S(2)}) collective-permute-start(bf16[256,384]{1,0:T(8,128)(2,1)S(1)} %collective-permute-done.span_2), channel_id=1, source_target_pairs={{0,32},{1,33},{2,34},{3,35},{4,36},{5,37},{6,38},{7,39},{8,40},{9,... | collective-permute-start | bytes 589832 | tf_op jit(solution)/shard_map/ppermute | solution.py:208
  49.9 26.2 %copy-start.1 = (bf16[512,192]{0,1:T(8,128)(2,1)S(1)}, bf16[512,192]{0,1:T(8,128)(2,1)}, u32[]{:S(2)}) copy-start(bf16[512,192]{0,1:T(8,128)(2,1)} %param.10) | copy-start | bytes 589828
